TPU v7x, 256 devices: a whole 4x4x8 slice. The times are simulated.
256 devices in a mesh: section: 8 (over z), vocab: 32 (over x, y, core).
Axes of the slice: x: 4, y: 4, z: 8, core: 2. Of those that a mesh axis runs over, the one named last changes fastest.
Arguments:
- section_hidden: bfloat16 [8, 256, 8192], P('section', None, 'vocab'), may hold values from -32 to 32
- norm_gain: float32 [8192], replicated, may hold values from 0.5 to 1.5
- head: bfloat16 [8192, 65536], P(None, ('section', 'vocab')), may hold values from -1 to 1
- teacher_logits: bfloat16 [256, 65536], P(None, ('section', 'vocab')), may hold values from -320 to 320
- exit_layer: int32 [256], replicated, may hold values from 9 to 79, as said below
- row_count: int32 [8], replicated, may hold values from 1 to 64, as said below
- row_index: int32 [8, 64], replicated, may hold values from 0 to 255, as said below
Outputs:
- exit_kl: float32 [8, 64], P('section')
- total_loss: float32 [], replicated
- grad_hidden: bfloat16 [8, 64, 8192], P('section', 'vocab')
Inputs may be any that keep to these rules, and one draw needn't show every extreme that they name: `row_index`: every token appears in exactly one used slot over all sections, that of the section of its exit layer; unused slots hold arbitrary token numbers. Some section uses all 64 slots in every draw. `row_count`: the counts add up to 256; some section's count is 64. `exit_layer`: A token scored at section s exits at layer 10 * (s + 1) - 1.
All inputs are finite; a program needn't handle non-finite values.
Results may differ from a plain program's by a relative error of at most 0.0093.
Values may be sent and summed in bfloat16 or wider, within the bound.
A program may use at most 128 MiB of HBM per device.

v0:
```python
import jax
import jax.numpy as jnp
from jax import lax
from jax.sharding import PartitionSpec as P

LAYERS = 80


EPS = 1e-05


def on_device(section_hidden, norm_gain, head, teacher_logits, exit_layer, row_count, row_index):
    section_count = lax.axis_size("section")
    vocab_count = lax.axis_size("vocab")
    device_count = section_count * vocab_count
    section_id = lax.axis_index("section")
    flat_id = lax.axis_index(("section", "vocab"))
    slot_count = row_index.shape[1]
    token_count = exit_layer.shape[0]
    slot_live = jnp.arange(slot_count, dtype=jnp.int32)[None, :] < row_count[:, None]
    own_index = lax.dynamic_index_in_dim(row_index, section_id, 0, keepdims=False)
    local_hidden = section_hidden[0]
    picked = jnp.take(local_hidden, own_index, axis=0)
    row_tokens = row_index.reshape(-1)
    row_live = slot_live.reshape(-1)
    teacher_rows = jnp.take(teacher_logits, row_tokens, axis=0)
    wide_rows = lax.all_gather(picked, "vocab", axis=1, tiled=True)
    all_rows = lax.all_gather(wide_rows, "section", axis=0, tiled=True)
    rows_f32 = all_rows.astype(jnp.float32)
    inv_rms = lax.rsqrt(jnp.mean(rows_f32 * rows_f32, axis=1, keepdims=True) + EPS)
    unit_rows = rows_f32 * inv_rms
    normed = (unit_rows * norm_gain).astype(jnp.bfloat16)
    student = jnp.dot(normed, head, preferred_element_type=jnp.float32)
    teacher = teacher_rows.astype(jnp.float32)
    teacher_local = jnp.max(teacher, axis=1)
    student_local = jnp.max(student, axis=1)
    teacher_top, student_top = lax.pmax((teacher_local, student_local), ("section", "vocab"))
    teacher_exp = jnp.exp(teacher - teacher_top[:, None])
    teacher_sum, cross_sum, student_sum = lax.psum(
        (
            jnp.sum(teacher_exp, axis=1),
            jnp.sum(teacher_exp * (teacher - student), axis=1),
            jnp.sum(jnp.exp(student - student_top[:, None]), axis=1),
        ),
        ("section", "vocab"),
    )
    teacher_lse = teacher_top + jnp.log(teacher_sum)
    student_lse = student_top + jnp.log(student_sum)
    kl_rows = jnp.where(row_live, cross_sum / teacher_sum - teacher_lse + student_lse, 0.0)
    weight = jnp.where(
        row_live, (jnp.take(exit_layer, row_tokens).astype(jnp.float32) + 1.0) / LAYERS, 0.0
    )
    total_loss = jnp.sum(weight * kl_rows) / token_count
    target_prob = jnp.exp(teacher - teacher_lse[:, None])
    dlogit = (weight[:, None] * (jnp.exp(student - student_lse[:, None]) - target_prob)).astype(
        jnp.bfloat16
    )
    rows_each = all_rows.shape[0] // device_count
    own_grad_normed = lax.psum_scatter(
        lax.dot_general(dlogit, head, (((1,), (1,)), ((), ())), preferred_element_type=jnp.float32),
        ("section", "vocab"),
        scatter_dimension=0,
        tiled=True,
    )
    own_unit = lax.dynamic_slice_in_dim(unit_rows, flat_id * rows_each, rows_each, 0)
    own_inv = lax.dynamic_slice_in_dim(inv_rms, flat_id * rows_each, rows_each, 0)
    scaled = norm_gain * own_grad_normed
    own_grad = (
        own_inv * (scaled - own_unit * jnp.mean(own_unit * scaled, axis=1, keepdims=True))
    ).astype(jnp.bfloat16)
    grad_hidden = own_grad.reshape(1, rows_each, own_grad.shape[1])
    exit_kl = lax.dynamic_index_in_dim(
        kl_rows.reshape(section_count, slot_count), section_id, 0, keepdims=True
    )
    return (exit_kl, total_loss, grad_hidden)


def solution(mesh):
    return jax.shard_map(
        on_device,
        mesh=mesh,
        in_specs=(
            P("section", None, "vocab"),
            P(),
            P(None, ("section", "vocab")),
            P(None, ("section", "vocab")),
            P(),
            P(),
            P(),
        ),
        out_specs=(P("section", None), P(), P("section", "vocab", None)),
        check_vma=False,
    )
```

profile of v0, /device:TPU:1, one launch (start us, length us, event | category | flops | bytes accessed | tf_op | source)
XLA Modules:
  0.0 633.8 jit_solution(18356008710446251764)
XLA Ops:
  7.2 0.7 fusion.19
  7.9 0.7 compare_and_fusion
  8.6 1.6 gather_fusion.1
  10.2 0.7 broadcast_select_fusion.2
  11.0 52.3 %all-gather.3.cloned.1.call-done = bf16[64,8192]{1,0:T(8,128)(2,1)} async-done(((bf16[64,256]{1,0:T(8,128)(2,1)}), bf16[64,8192]{1,0:T(8,128)(2,1)}) %all-gather.3.cloned.1.call-update) | async-done | bytes 1048592 | tf_op jit(solution)/shard_map/all_gather | solution.py:27
  63.4 0.8 reshape.149
  64.1 0.8 reshape.148
  64.9 2.0 gather_fusion
  66.9 0.1 copy.12
  67.0 3.6 gather_fusion.2
  70.7 0.7 iota_compare_fusion
  71.6 86.7 %all-gather.5.cloned.1.call-done = bf16[512,8192]{1,0:T(8,128)(2,1)} async-done(((bf16[64,8192]{1,0:T(8,128)(2,1)}), bf16[512,8192]{1,0:T(8,128)(2,1)}) %all-gather.5.cloned.1.call-update) | async-done | bytes 8388624 | tf_op jit(solution)/shard_map/all_gather | solution.py:28
  158.3 5.1 fusion
  163.4 7.6 %fusion.21 = (f32[512]{0:T(512)S(1)}, f32[512,256]{0,1:T(8,128)S(1)}) fusion(bf16[8192,256]{1,0:T(8,128)(2,1)} %param.9, f32[8192]{0:T(1024)} %param.8, f32[512]{0:T(512)S(1)} %add_rsqrt_fusion, bf16[512,8192]{1,0:T(8,128)(2,1)} %all-gather.5.cloned.1.call-done), kind=kOutput, calls=%fused_computation.53 | convolution fusion | flops 2164391424 | bytes 13144064 | tf_op jit(solution)/shard_map/dot_general | solution.py:33
  171.0 76.4 %all-reduce.2 = (f32[512]{0:T(512)S(1)}, f32[512]{0:T(512)S(1)}) all-reduce(f32[512]{0:T(512)S(1)} %get-tuple-element.16, bf16[512]{0:T(512)(128)(2,1)S(1)} %fusion.16), channel_id=1, replica_groups=mesh['section'=8,'vocab'=32] {'section','vocab'}, use_global_device_ids=true, to_apply=%region_8.9 | all-reduce | flops 1024 | bytes 7168 | tf_op jit(solution)/shard_map/pmax | solution.py:37
  247.4 0.2 fusion.6
  247.6 72.8 %all-reduce.1 = (f32[512]{0:T(512)S(1)}, f32[512]{0:T(512)S(1)}, f32[512]{0:T(512)S(1)}) all-reduce(f32[512]{0:T(512)S(1)} %get-tuple-element.4, f32[512]{0:T(512)S(1)} %get-tuple-element.5, f32[512]{0:T(512)S(1)} %get-tuple-element.3), channel_id=1, replica_groups=mesh['section'=8,'vocab'=32] {'section','vocab'}, use_global_device_ids=true, to_apply=%region_10.11 | all-reduce | flops 1536 | bytes 12288 | tf_op jit(solution)/shard_map/psum | solution.py:39
  320.5 0.6 multiply_reduce_fusion.1
  321.1 10.4 %fusion.11 = f32[512,8192]{1,0:T(8,128)} fusion(bf16[8192,256]{1,0:T(8,128)(2,1)} %param.9, f32[512,256]{0,1:T(8,128)S(1)} %get-tuple-element.17, f32[512]{0:T(512)S(1)} %get-tuple-element.14, f32[512]{0:T(512)S(1)} %get-tuple-element.15, f32[512]{0:T(512)S(1)} %get-tuple-element.12, bf16[512,256]{0,1:T(8,128)(2,1)S(1)} %copy.12, ...), kind=kOutput, calls=%fused_computation.21 | convolution fusion | flops 2148401152 | bytes 21764608 | tf_op jit(solution)/shard_map/dot_general | solution.py:60
  332.3 0.5 constant_dynamic-slice_fusion
  332.9 12.2 %convert_multiply_fusion = f32[512,8192]{1,0:T(8,128)} fusion(bf16[512,8192]{1,0:T(8,128)(2,1)} %all-gather.5.cloned.1.call-done, f32[512]{0:T(512)S(1)} %add_rsqrt_fusion), kind=kLoop, calls=%fused_computation.3 | loop fusion | flops 8388608 | bytes 25167872 | tf_op jit(solution)/shard_map/mul | solution.py:31
  345.1 278.1 %all-reduce.5.cloned.1.call-done = f32[512,8192]{1,0:T(8,128)} async-done(((f32[512,8192]{1,0:T(8,128)}), f32[512,8192]{1,0:T(8,128)}) %all-reduce.5.cloned.1.call-update) | async-done | bytes 16777232
  623.2 1.2 multiply_reduce_fusion
  624.4 1.8 fusion.18
  (20 shorter events, 0.5 us)
Async XLA Ops:
  7.2 57.7 %copy-start = (bf16[256,256]{1,0:T(8,128)(2,1)S(1)}, bf16[256,256]{1,0:T(8,128)(2,1)}, u32[]{:S(2)}) copy-start(bf16[256,256]{1,0:T(8,128)(2,1)} %param.10) | copy-start | bytes 393220
  7.2 56.1 %all-gather.3.cloned.1.call-start = ((), (), s32[]{:S(2)}) async-start(), calls=%async_computation | async-start | bytes 1081344 | tf_op jit(solution)/shard_map/all_gather | solution.py:27
  10.9 147.3 %all-gather.5.cloned.1.call-start = ((), (), s32[]{:S(2)}) async-start(), calls=%async_computation.1 | async-start | bytes 9437184 | tf_op jit(solution)/shard_map/all_gather | solution.py:28
  63.3 559.9 %all-reduce.5.cloned.1.call-start = ((), (), s32[]{:S(2)}) async-start(), calls=%async_computation.2 | async-start | bytes 33554432
  331.5 291.7 %copy-start.1 = (f32[8192]{0:T(1024)S(1)}, f32[8192]{0:T(1024)}, u32[]{:S(2)}) copy-start(f32[8192]{0:T(1024)} %param.8) | copy-start | bytes 98308
Sparse Core Ops, SparseCore 0:
  11.1 52.1 all-gather.2
  65.1 93.1 all-gather.4
  331.6 291.5 all-reduce.4
where the time goes:
time: 635 us; the launch traced here: 634 us
  waiting for transfers between devices  417 us (66%)
  blocking collectives  149 us (23%)
  other arithmetic  24.1 us (4%)
  matrix products  18 us (3%)
  between operations  15.6 us (2%)
  local copies, waits for them, and re-layouts  9.6 us (2%)
    unnamed x4, waiting for transfers between devices  278 us
    all_gather x1, waiting for transfers between devices, on_device(): all_rows = lax.all_gather(wide_rows, 'section', axis=0, tiled=True)  86.7 us
    pmax x1, blocking collectives, on_device(): lax.pmax((teacher_local, student_local), ('section', 'vocab'))  76.4 us
    psum x1, blocking collectives, on_device(): lax.psum((jnp.sum(teacher_exp, axis=1), jnp.sum(teacher_exp * (teacher -...  72.8 us
    all_gather x1, waiting for transfers between devices, on_device(): wide_rows = lax.all_gather(picked, 'vocab', axis=1, tiled=True)  52.3 us
  transfers between devices with their start and end apart: 3, of which 3 were waited for; matrix products, arithmetic and copies ran while one was open for 3% of the time, Pallas kernels for 0%

commit v1 on v0

v1 whole, which is shorter than its diff:
```python
import functools

import jax
import jax.numpy as jnp
from jax import lax
from jax.experimental import pallas as pl
from jax.experimental.pallas import tpu as pltpu
from jax.sharding import PartitionSpec as P

LAYERS = 80
EPS = 1e-05
F32 = jnp.float32
BF16 = jnp.bfloat16
MESH = pl.DeviceIdType.MESH

NZ, NX, NY, NC = 8, 4, 4, 2
NV = NX * NY * NC
TOK = 256
SLOTS = 64
FC = 256
HALF = TOK // 2
QUART = TOK // 4
OFFS = (0, 1, -1, 2)
PLANE = [(a, b) for a in OFFS for b in OFFS]
PEERS_XY = [o for o in PLANE if o != (0, 0)]
PEERS_Z = (1, -1, 2, -2, 3, -3, 4)
FAR = [(2, 2), (2, 1), (1, 2), (2, -1), (-1, 2), (2, 0), (0, 2), (1, 1), (-1, 1), (1, -1), (-1, -1), (0, 1), (1, 0), (0, -1), (-1, 0), (0, 0)]


class Names:
    def __init__(self):
        self.table = {}

    def __call__(self, *key):
        return self.table.setdefault(key, len(self.table))


def all_names():
    n = Names()
    for d in PEERS_Z:
        n("zrow", d), n("zt", d), n("zs", d), n("zg", d)
    for o in PEERS_XY:
        n("xt", o), n("xs", o), n("tr", o)
    for k in ("ct", "cs", "cr"):
        n(k)
    for p in (0, 1):
        for ph in ("g", "r"):
            for d in OFFS + ("one",):
                for s in (0, 1):
                    n(ph, p, d, "f", s), n(ph, p, d, "h", s)
    for o in PLANE:
        for p in (0, 1):
            n("cg", o, p)
        n("cp", o)
    return n


NAMES = all_names()


def dot(a, b, dims):
    return lax.dot_general(a, b, (dims, ((), ())), preferred_element_type=F32)


def kernel(
    hidden_ref, gain_ref, head_ref, teacher_ref, layer_ref, count_ref, index_ref,
    kl_ref, loss_ref, grad_ref,
    head, rows, zrow, zt, zs, xt, xs, ct, cs,
    hot, cross_out, cross_in, part_sum, half_out, half_in, full_out, full_in,
    z_out, z_in, tr_out, tr_in, tr_side,
    stu, head_sem, send_sem, recv_sem,
):
    z = lax.axis_index("section")
    v = lax.axis_index("vocab")
    x, y, c = v // (NY * NC), lax.rem(v // NC, NY), lax.rem(v, NC)
    other = 1 - c

    def vid(dx, dy, core):
        return (lax.rem(x + dx + NX, NX) * NY + lax.rem(y + dy + NY, NY)) * NC + core

    def qid(dx, dy):
        return lax.rem(x + dx + NX, NX) * NY + lax.rem(y + dy + NY, NY)

    def zid(dz):
        return lax.rem(z + dz + NZ, NZ)

    def to_xy(dx, dy):
        return (z, vid(dx, dy, c))

    def to_z(dz):
        return (zid(dz), v)

    sibling = (z, vid(0, 0, other))
    pending = []

    def copy(name, src, dst, target):
        k = NAMES.table[name]
        return pltpu.make_async_remote_copy(
            src_ref=src, dst_ref=dst, send_sem=send_sem.at[k], recv_sem=recv_sem.at[k],
            device_id=target, device_id_type=MESH)

    def send(name, src, dst, target):
        cp = copy(name, src, dst, target)
        cp.start()
        pending.append(cp)

    def got(name, dst):
        copy(name, dst, dst, sibling).wait_recv()

    barrier = pltpu.get_barrier_semaphore()
    partners = [sibling] + [to_z(d) for d in PEERS_Z] + [to_xy(*o) for o in PEERS_XY]
    for t in partners:
        pl.semaphore_signal(barrier, inc=1, device_id=t, device_id_type=MESH)
    loads = [pltpu.make_async_copy(head_ref.at[pl.ds(8 * i, 8)], head.at[pl.ds(8 * i, 8)], head_sem.at[i]) for i in range(4)]
    for cp in loads:
        cp.start()

    tok_iota = lax.broadcasted_iota(jnp.int32, (TOK, SLOTS), 0)
    slot_iota = lax.broadcasted_iota(jnp.int32, (1, SLOTS), 1)
    own_row = index_ref[pl.ds(z, 1), :]
    pick = (tok_iota == own_row).astype(F32).astype(BF16)
    zrow[z] = dot(pick, hidden_ref[0], ((0,), (0,))).astype(BF16)
    tea = teacher_ref[...].astype(F32).T
    top = jnp.max(tea, axis=0, keepdims=True)
    zt[z, 0:1] = top
    zt[z, 1:2] = jnp.sum(jnp.exp(tea - top), axis=0, keepdims=True)
    pl.semaphore_wait(barrier, len(partners))

    for d in PEERS_Z:
        send(("zrow", d), zrow.at[z], zrow.at[z], to_z(d))
    for d in PEERS_Z:
        send(("zt", d), zt.at[z], zt.at[z], to_z(d))

    for s in range(NZ):
        live_row = jnp.where(slot_iota < count_ref[s], index_ref[s : s + 1, :], -1)
        hot[s] = (tok_iota == live_row).astype(F32).astype(BF16)

    for d in PEERS_Z:
        got(("zrow", d), zrow.at[z])
    mine = dot(hot[0], zrow[0], ((1,), (0,)))
    for s in range(1, NZ):
        mine = mine + dot(hot[s], zrow[s], ((1,), (0,)))
    rows[v] = mine.astype(BF16)
    square = mine * mine
    square = (square[:, :128] + square[:, 128:]).T
    for d in PEERS_Z:
        got(("zt", d), zt.at[z])

    def merge(buf, n, at):
        m = buf[0, at : at + 1]
        for i in range(1, n):
            m = jnp.maximum(m, buf[i, at : at + 1])
        t = jnp.zeros_like(m)
        for i in range(n):
            t = t + buf[i, at + 1 : at + 2] * jnp.exp(buf[i, at : at + 1] - m)
        return m, t

    def total(buf, n, at):
        t = buf[0, at : at + 1]
        for i in range(1, n):
            t = t + buf[i, at : at + 1]
        return t

    q_me = qid(0, 0)
    m, t = merge(zt, NZ, 0)
    xt[q_me, 0:1] = m
    xt[q_me, 1:2] = t
    xt[q_me, 2:3] = jnp.sum(square, axis=0, keepdims=True)
    for o in PEERS_XY:
        send(("xt", o), xt.at[q_me], xt.at[q_me], to_xy(*o))

    def off(p, d1, d2):
        return (d1, d2) if p == 0 else (d2, d1)

    def axis1(p, d):
        return to_xy(d, 0) if p == 0 else to_xy(0, d)

    def axis2(p, d):
        return to_xy(0, d) if p == 0 else to_xy(d, 0)

    def block(p, o, h=None):
        if h is None:
            return rows.at[vid(*o, c), pl.ds(HALF * p, HALF)]
        return rows.at[vid(*o, c), pl.ds(HALF * p + QUART * h, QUART)]

    def relay(p, o):
        send(("cg", o, p), block(p, o), block(p, o), sibling)

    def spread(p, d1):
        o = off(p, d1, 0)
        send(("g", p, d1, "f", 0), block(p, o), block(p, o), axis2(p, 1))
        send(("g", p, d1, "f", 1), block(p, o), block(p, o), axis2(p, -1))

    sides = ((0, -1, 1), (1, 1, -1))
    for p in (0, 1):
        send(("g", p, "one", "f", 0), block(p, (0, 0)), block(p, (0, 0)), axis1(p, 1))
        send(("g", p, "one", "f", 1), block(p, (0, 0)), block(p, (0, 0)), axis1(p, -1))
    for p in (0, 1):
        relay(p, (0, 0))
    for p in (0, 1):
        spread(p, 0)
    for s, frm, to in sides:
        for p in (0, 1):
            o = off(p, frm, 0)
            got(("g", p, "one", "f", s), block(p, o))
            send(("g", p, "one", "h", s), block(p, o, s), block(p, o, s), axis1(p, to))
            spread(p, frm)
            relay(p, o)

    for o in PEERS_XY:
        got(("xt", o), xt.at[q_me])
    m, t = merge(xt, NX * NY, 0)
    ct[c, 0:1] = m
    ct[c, 1:2] = t
    ct[c, 2:3] = total(xt, NX * NY, 2)
    send(("ct",), ct.at[c], ct.at[c], sibling)
    for p in (0, 1):
        o = off(p, 2, 0)
        for s in (0, 1):
            got(("g", p, "one", "h", s), block(p, o, s))
        spread(p, 2)
        relay(p, o)
    got(("ct",), ct.at[c])
    m, t = merge(ct, NC, 0)
    lse_t = m + jnp.log(t)
    inv = lax.rsqrt(total(ct, NC, 2) / (NV * FC) + EPS)
    inv_col = jnp.broadcast_to(inv, (128, TOK)).T
    inv_wide = jnp.concatenate([inv_col, inv_col], axis=1)
    prob = jnp.exp(tea - lse_t)
    for cp in loads:
        cp.wait()

    stu[...] = jnp.zeros_like(stu)

    def score(chunk):
        normed = (rows[chunk].astype(F32) * inv_wide * gain_ref[pl.ds(chunk, 1), :]).astype(BF16)
        stu[...] += dot(normed, head[chunk], ((1,), (0,)))

    score(vid(0, 0, c))
    done = {}

    def arrived(p, o):
        relay(p, o)
        done[o] = done.get(o, 0) + 1
        if done[o] == 2:
            score(vid(*o, c))

    for d1 in (1, -1, 2):
        for p in (0, 1):
            done[off(p, d1, 0)] = done.get(off(p, d1, 0), 0) + 1
    for d1 in OFFS:
        for s, frm, to in sides:
            for p in (0, 1):
                o = off(p, d1, frm)
                got(("g", p, d1, "f", s), block(p, o))
                send(("g", p, d1, "h", s), block(p, o, s), block(p, o, s), axis2(p, to))
                arrived(p, o)
    for d1 in OFFS:
        for p in (0, 1):
            o = off(p, d1, 2)
            for s in (0, 1):
                got(("g", p, d1, "h", s), block(p, o, s))
            arrived(p, o)
    for o in sorted(PLANE, key=lambda o: (2 in o, o != (0, 0))):
        for p in (0, 1):
            got(("cg", o, p), block(p, o))
        score(vid(*o, other))

    student = stu[...].T
    m = jnp.max(student, axis=0, keepdims=True)
    cs[c, 0:1] = m
    cs[c, 1:2] = jnp.sum(jnp.exp(student - m), axis=0, keepdims=True)
    cs[c, 2:3] = jnp.sum(prob * (tea - student), axis=0, keepdims=True)
    send(("cs",), cs.at[c], cs.at[c], sibling)
    got(("cs",), cs.at[c])
    m, t = merge(cs, NC, 0)
    zs[z, 0:1] = m
    zs[z, 1:2] = t
    zs[z, 2:3] = total(cs, NC, 2)
    for d in PEERS_Z:
        send(("zs", d), zs.at[z], zs.at[z], to_z(d))
    for d in PEERS_Z:
        got(("zs", d), zs.at[z])
    m, t = merge(zs, NZ, 0)
    xs[q_me, 0:1] = m
    xs[q_me, 1:2] = t
    xs[q_me, 2:3] = total(zs, NZ, 2)
    for o in PEERS_XY:
        send(("xs", o), xs.at[q_me], xs.at[q_me], to_xy(*o))
    for o in PEERS_XY:
        got(("xs", o), xs.at[q_me])
    m, t = merge(xs, NX * NY, 0)
    lse_s = m + jnp.log(t)
    kl = total(xs, NX * NY, 2) - lse_t + lse_s
    weight = (layer_ref[...].astype(F32) + 1.0) / LAYERS
    dlogit = (weight * (jnp.exp(student - lse_s) - prob)).T.astype(BF16)

    def part(chunk):
        return dot(dlogit, head[chunk], ((1,), (1,)))

    def own(o):
        return PLANE.index(o)

    def give(p, d, ph_axis, h, value):
        half_out[p, d, h] = value.astype(BF16)
        send(("r", p, OFFS[d] if d < 4 else "one", "h", h), half_out.at[p, d, h], half_in.at[p, d, h], ph_axis(p, 1 if h == 0 else -1))

    def settle(o):
        i = own(o)
        got(("cp", o), cross_in.at[i])
        part_sum[i] = part_sum[i] + cross_in[i].astype(F32)
        for p in (0, 1):
            d1, d2 = o if p == 0 else o[::-1]
            if d2 == 2:
                for h in (0, 1):
                    give(p, OFFS.index(d1), axis2, h, part_sum[i, pl.ds(HALF * p + QUART * h, QUART)])

    lag = 3
    for k, o in enumerate(FAR):
        i = own(o)
        cross_out[i] = part(vid(*o, other)).astype(BF16)
        send(("cp", o), cross_out.at[i], cross_in.at[i], sibling)
        part_sum[i] = part(vid(*o, c))
        if k >= lag:
            settle(FAR[k - lag])
    for o in FAR[-lag:]:
        settle(o)

    def pass_on(p, d, axis, near):
        key = OFFS[d] if d < 4 else "one"
        for s in (0, 1):
            got(("r", p, key, "h", s), half_in.at[p, d, s])
            base = QUART * s
            rest = QUART * (1 - s)
            full_out[p, d, s, pl.ds(base, QUART)] = (near(s, base) + half_in[p, d, s].astype(F32)).astype(BF16)
            full_out[p, d, s, pl.ds(rest, QUART)] = near(s, rest).astype(BF16)
            send(("r", p, key, "f", s), full_out.at[p, d, s], full_in.at[p, d, s], axis(p, 1 if s == 0 else -1))

    def collect(p, d):
        key = OFFS[d] if d < 4 else "one"
        for s in (0, 1):
            got(("r", p, key, "f", s), full_in.at[p, d, s])
        return full_in[p, d, 0].astype(F32) + full_in[p, d, 1].astype(F32)

    order = (3, 1, 2, 0)
    for d in order:
        for p in (0, 1):
            def near(s, base, p=p, d=d):
                return part_sum[own(off(p, OFFS[d], 1 if s == 0 else -1)), pl.ds(HALF * p + base, QUART)]
            pass_on(p, d, axis2, near)
    for d in order:
        for p in (0, 1):
            i = own(off(p, OFFS[d], 0))
            part_sum[i, pl.ds(HALF * p, HALF)] = part_sum[i, pl.ds(HALF * p, HALF)] + collect(p, d)
            if d == 3:
                for h in (0, 1):
                    give(p, 4, axis1, h, part_sum[i, pl.ds(HALF * p + QUART * h, QUART)])
    for p in (0, 1):
        def near(s, base, p=p):
            return part_sum[own(off(p, 1 if s == 0 else -1, 0)), pl.ds(HALF * p + base, QUART)]
        pass_on(p, 4, axis1, near)

    hot_own = hot[z]
    two = lax.broadcasted_iota(jnp.int32, (16, SLOTS), 0) + 2 * v == lax.broadcasted_iota(jnp.int32, (16, SLOTS), 1)
    sel_f = dot(two.astype(F32).astype(BF16), hot_own, ((1,), (1,)))
    sel = sel_f.astype(BF16)
    inv_two = jnp.sum(sel_f[0:2] * inv, axis=1, keepdims=True)
    for i in range(NV):
        tr_side[1, i] = dot(sel, rows[i], ((1,), (0,)))[0:2] * inv_two
    kl_col = jnp.broadcast_to(kl, (128, TOK)).T
    kl_ref[...] = jnp.sum(hot_own.astype(F32) * kl_col[:, :SLOTS], axis=0, keepdims=True)
    loss_ref[...] = jnp.sum(weight * kl, axis=1, keepdims=True) / TOK

    i0 = own((0, 0))
    whole = []
    for p in (0, 1):
        whole.append((part_sum[i0, pl.ds(HALF * p, HALF)] + collect(p, 4)).astype(BF16))
    whole = jnp.concatenate(whole, axis=0)

    for d in PEERS_Z:
        k = PEERS_Z.index(d)
        z_out[k] = dot(hot[zid(d)], whole, ((0,), (0,))).astype(BF16)
        send(("zg", d), z_out.at[k], z_in.at[k], to_z(d))
    grads = dot(hot_own, whole, ((0,), (0,)))
    for d in PEERS_Z:
        k = PEERS_Z.index(d)
        got(("zg", d), z_in.at[k])
        grads = grads + z_in[k].astype(F32)
    for q in range(NX * NY):
        for cc in range(NC):
            j = (q * NC + cc) * 2
            tr_out[q, cc] = grads[j : j + 2]
    for o in PEERS_XY:
        send(("tr", o), tr_out.at[qid(*o)], tr_in.at[q_me], to_xy(*o))
    tr_in[q_me] = tr_out[q_me]
    for o in PEERS_XY:
        got(("tr", o), tr_in.at[q_me])
    send(("cr",), tr_in.at[:, other], tr_side.at[0, pl.ds(0, 16)], sibling)
    got(("cr",), tr_side.at[0, pl.ds(0, 16)])
    both = []
    acc = jnp.zeros((2, FC), F32)
    for q in range(NX * NY):
        for cc in range(NC):
            i = q * NC + cc
            dn = jnp.where(c == cc, tr_in[q, cc], tr_side[0, q]) * gain_ref[i : i + 1, :]
            both.append(dn)
            acc = acc + dn * tr_side[1, i]
    mean = jnp.sum(acc, axis=1, keepdims=True) / (NV * FC)
    for i in range(NV):
        grad_ref[0, :, FC * i : FC * (i + 1)] = (inv_two * (both[i] - tr_side[1, i] * mean)).astype(BF16)
    for cp in pending:
        cp.wait_send()


def on_device(section_hidden, norm_gain, head, teacher_logits, exit_layer, row_count, row_index):
    vmem = pl.BlockSpec(memory_space=pltpu.VMEM)
    n = len(NAMES.table)
    exit_kl, loss, grad = pl.pallas_call(
        kernel,
        out_shape=(
            jax.ShapeDtypeStruct((1, SLOTS), F32),
            jax.ShapeDtypeStruct((1, 1), F32),
            jax.ShapeDtypeStruct((1, 2, NV * FC), BF16),
        ),
        in_specs=[vmem, vmem, pl.BlockSpec(memory_space=pl.ANY), vmem, vmem, pl.BlockSpec(memory_space=pltpu.SMEM), vmem],
        out_specs=(vmem, vmem, vmem),
        scratch_shapes=[
            pltpu.VMEM((NV, FC, TOK), BF16),
            pltpu.VMEM((NV, TOK, FC), BF16),
            pltpu.VMEM((NZ, SLOTS, FC), BF16),
            pltpu.VMEM((NZ, 4, TOK), F32),
            pltpu.VMEM((NZ, 4, TOK), F32),
            pltpu.VMEM((NX * NY, 4, TOK), F32),
            pltpu.VMEM((NX * NY, 4, TOK), F32),
            pltpu.VMEM((NC, 4, TOK), F32),
            pltpu.VMEM((NC, 4, TOK), F32),
            pltpu.VMEM((NZ, TOK, SLOTS), BF16),
            pltpu.VMEM((16, TOK, FC), BF16),
            pltpu.VMEM((16, TOK, FC), BF16),
            pltpu.VMEM((16, TOK, FC), F32),
            pltpu.VMEM((2, 5, 2, QUART, FC), BF16),
            pltpu.VMEM((2, 5, 2, QUART, FC), BF16),
            pltpu.VMEM((2, 5, 2, HALF, FC), BF16),
            pltpu.VMEM((2, 5, 2, HALF, FC), BF16),
            pltpu.VMEM((7, SLOTS, FC), BF16),
            pltpu.VMEM((7, SLOTS, FC), BF16),
            pltpu.VMEM((16, 2, 2, FC), F32),
            pltpu.VMEM((16, 2, 2, FC), F32),
            pltpu.VMEM((2, NV, 2, FC), F32),
            pltpu.VMEM((TOK, 256), F32),
            pltpu.SemaphoreType.DMA((4,)),
            pltpu.SemaphoreType.DMA((n,)),
            pltpu.SemaphoreType.DMA((n,)),
        ],
        compiler_params=pltpu.CompilerParams(collective_id=0, has_side_effects=True, vmem_limit_bytes=48 * 2**20),
        name="exit_loss",
    )(
        section_hidden,
        norm_gain.reshape(NV, FC),
        head.reshape(NV, FC, head.shape[1]),
        teacher_logits,
        exit_layer.reshape(1, TOK),
        row_count,
        row_index,
    )
    return exit_kl, loss.reshape(()), grad


def solution(mesh):
    return jax.shard_map(
        on_device,
        mesh=mesh,
        in_specs=(
            P("section", None, "vocab"),
            P(),
            P(None, ("section", "vocab")),
            P(None, ("section", "vocab")),
            P(),
            P(),
            P(),
        ),
        out_specs=(P("section", None), P(), P("section", "vocab", None)),
        check_vma=False,
    )
```

time: 635 us -> 101 us (0.16)
  waiting for transfers between devices: 417 us -> 0 us
  blocking collectives: 149 us -> 0 us
  Pallas kernels: 0 us -> 90.6 us
  other arithmetic: 24.1 us -> 0 us
  matrix products: 18 us -> 0 us
  between operations: 15.6 us -> 2.48 us
    unnamed x4 -> x0, waiting for transfers between devices: 278 us -> none
    all_gather x2 -> x0, waiting for transfers between devices: 139 us -> none  [the longest x1 86.7 us: on_device(): all_rows = lax.all_gather(wide_rows, 'section', axis=0, tiled=True)]
    pallas_call x0 -> x1, Pallas kernels: none -> 90.6 us  [on_device(): pl.pallas_call(kernel, out_shape=(jax.ShapeDtypeStruct((1, SLOTS), F32),...]
    pmax x1 -> x0, blocking collectives: 76.4 us -> none  [on_device(): lax.pmax((teacher_local, student_local), ('section', 'vocab'))]
    psum x1 -> x0, blocking collectives: 72.8 us -> none  [on_device(): lax.psum((jnp.sum(teacher_exp, axis=1), jnp.sum(teacher_exp * (teacher -...]
    dot_general x2 -> x0, matrix products: 18 us -> none  [the longest x1 10.4 us: on_device(): lax.dot_general(dlogit, head, (((1,), (1,)), ((), ())), preferred_element...]
    mul x1 -> x0, other arithmetic: 12.2 us -> none  [on_device(): unit_rows = rows_f32 * inv_rms]
    gather x4 -> x0, local copies, waits for them, and re-layouts: 7.3 us -> none  [the longest x1 3.62 us: on_device(): jnp.take(exit_layer, row_tokens).astype(jnp.float32) + 1.0]
  transfers between devices with their start and end apart: 3 -> 0, of which waited for: 3 -> 0; matrix products, arithmetic and copies ran while one was open for 3% -> 0% of each run, Pallas kernels for 0% -> 0%
where the time goes in v1:
time: 101 us
  Pallas kernels  90.6 us (90%)
  local copies, waits for them, and re-layouts  7.91 us (8%)
  between operations  2.48 us (2%)
    pallas_call x1, Pallas kernels, on_device(): pl.pallas_call(kernel, out_shape=(jax.ShapeDtypeStruct((1, SLOTS), F32),...  90.6 us
    unnamed x14, local copies, waits for them, and re-layouts  7.14 us

profile of v1, /device:TPU:1, one launch (start us, length us, event | category | flops | bytes accessed | tf_op | source)
XLA Modules:
  0.0 101.0 jit_solution(8707677421169381273)
XLA Ops:
  0.6 0.8 reshape.18.gain_ref
  1.4 0.0 copy-start
  1.4 2.2 %copy-done = bf16[8192,256]{1,0:T(8,128)(2,1)S(1)} copy-done((bf16[8192,256]{1,0:T(8,128)(2,1)S(1)}, bf16[8192,256]{1,0:T(8,128)(2,1)}, u32[]{:S(2)}) %copy-start) | copy-done | bytes 4194328
  3.6 0.0 copy-start.1
  3.6 0.9 copy-done.1
  4.5 0.0 copy-start.2
  4.5 0.9 copy-done.2
  5.4 0.0 copy-start.3
  5.4 0.7 copy-done.3
  6.1 0.0 copy-start.4
  6.1 0.7 copy-done.4
  6.8 0.0 copy-start.5
  6.8 0.7 copy-done.5
  7.4 90.6 %exit_loss.1 = (f32[1,64]{1,0:T(1,128)S(1)}, f32[1,1]{1,0:T(1,128)}, bf16[1,2,8192]{2,1,0:T(2,128)(2,1)S(1)}) custom-call(bf16[1,256,256]{2,1,0:T(8,128)(2,1)S(1)} %copy-done.1, f32[32,256]{1,0:T(8,128)S(1)} %reshape.18.gain_ref, bf16[32,256,256]{2,1,0:T(8,128)(2,1)S(1)} %bitcast.3, bf16[256,256]{1,0:T(8,128)(2,1)S(1)} %copy-done.2, s32[1,256]{1,0:T(1,128)S(1)} %bitcast.4, ...), custom_call_target="tpu_custom_call" | custom-call | tf_op jit(solution)/shard_map/exit_loss/pallas_call | solution.py:418
  98.1 0.5 copy.13
  99.3 0.6 copy.15
Async XLA Ops:
  1.4 2.2 %copy-start = (bf16[8192,256]{1,0:T(8,128)(2,1)S(1)}, bf16[8192,256]{1,0:T(8,128)(2,1)}, u32[]{:S(2)}) copy-start(bf16[8192,256]{1,0:T(8,128)(2,1)} %param.9) | copy-start | bytes 12582916
  3.6 0.9 copy-start.1
  4.5 0.9 copy-start.2
  5.4 0.7 copy-start.3
  6.1 0.7 copy-start.4
  6.8 0.7 copy-start.5

commit v2 on v0

v2 whole, which is shorter than its diff:
```python
import jax
import jax.numpy as jnp
from jax import lax
from jax.experimental import pallas as pl
from jax.experimental.pallas import tpu as pltpu
from jax.sharding import PartitionSpec as P

LAYERS = 80
EPS = 1e-05
F32 = jnp.float32
BF16 = jnp.bfloat16
MESH = pl.DeviceIdType.MESH

NZ, NX, NY, NC = 8, 4, 4, 2
NV = NX * NY * NC
TOK = 256
SLOTS = 64
FC = 256
HF = FC // 2
HT = TOK // 2
OFFS = (0, 1, -1, 2)
PLANE = [(a, b) for a in OFFS for b in OFFS]
PEERS_XY = sorted((o for o in PLANE if o != (0, 0)), key=lambda o: -abs(o[0]) - abs(o[1]))
PEERS_Z = (4, 3, -3, 2, -2, 1, -1)
FAR = [(2, 2), (2, 1), (1, 2), (2, -1), (-1, 2), (2, 0), (0, 2), (1, 1), (-1, 1), (1, -1), (-1, -1), (0, 1), (1, 0), (0, -1), (-1, 0), (0, 0)]


RING_G = (0, 1, -1)
RING_R = (0, 1, -1)


def all_names():
    names = ["z0", "z1", "zt", "xt", "ct", "cs", "zs", "xs", "zg0", "zg1", "tr", "cr"]
    names += [("ring", p, d, k) for p in (0, 1) for d in OFFS + ("one",) for k in range(3)]
    names += [("core", o) for o in PLANE]
    return {k: i for i, k in enumerate(names)}


NAMES = all_names()
GROUPS = {k: i for i, k in enumerate(["z0", "z1", "zt", "xt", "ct", "cs", "zs", "xs", "zg0", "zg1", "tr", "cr", "g", "r", "cg", "cr2"])}


def dot(a, b, dims):
    return lax.dot_general(a, b, (dims, ((), ())), preferred_element_type=F32)


def kernel(
    hidden_hbm, gain_hbm, head_hbm, teacher_hbm, layer_hbm, count_hbm, index_hbm,
    out_ref,
    hidden_ref, gain_ref, teacher_ref, layer_ref, count_ref, index_ref, head,
    rows, zrow, zt, zs, xt, xs, ct, cs,
    hot, cross_out, cross_in, part_sum, half_out, half_in, full_out, full_in,
    z_out, z_in, tr_out, tr_in, tr_side, unit_ref,
    stu, load_sem, head_sem, send_sem, recv_sem,
):
    z = lax.axis_index("section")
    v = lax.axis_index("vocab")
    x, y, c = v // (NY * NC), lax.rem(v // NC, NY), lax.rem(v, NC)
    other = 1 - c

    def qid(dx, dy):
        return lax.rem(x + dx + NX, NX) * NY + lax.rem(y + dy + NY, NY)

    def vid(dx, dy, core):
        return qid(dx, dy) * NC + core

    def zid(dz):
        return lax.rem(z + dz + NZ, NZ)

    def to_xy(dx, dy):
        return (z, vid(dx, dy, c))

    def to_z(dz):
        return (zid(dz), v)

    sibling = (z, vid(0, 0, other))

    def send(group, name, src, dst, target):
        pltpu.make_async_remote_copy(
            src_ref=src, dst_ref=dst, send_sem=send_sem.at[GROUPS[group]], recv_sem=recv_sem.at[NAMES[name]],
            device_id=target, device_id_type=MESH).start()

    def got(name, dst):
        pltpu.make_async_copy(dst, dst, recv_sem.at[NAMES[name]]).wait()

    def sent(group, src):
        pltpu.make_async_copy(src, src, send_sem.at[GROUPS[group]]).wait()

    def gain(chunk):
        return jnp.concatenate([gain_ref[pl.ds(2 * chunk, 1), :], gain_ref[pl.ds(2 * chunk + 1, 1), :]], axis=1)

    barrier = pltpu.get_barrier_semaphore()
    partners = [to_z(d) for d in PEERS_Z] + [to_xy(*o) for o in PEERS_XY] + [sibling]
    for t in partners:
        pl.semaphore_signal(barrier, inc=1, device_id=t, device_id_type=MESH)
    small = [(index_hbm, index_ref), (hidden_hbm, hidden_ref), (teacher_hbm, teacher_ref), (count_hbm, count_ref), (gain_hbm, gain_ref), (layer_hbm, layer_ref)]
    small = [pltpu.make_async_copy(a, b, load_sem.at[i]) for i, (a, b) in enumerate(small)]
    loads = [pltpu.make_async_copy(head_hbm.at[pl.ds(8 * i, 8)], head.at[pl.ds(8 * i, 8)], head_sem.at[i]) for i in range(4)]
    for cp in small + loads:
        cp.start()
    for cp in small:
        cp.wait()

    tok_iota = lax.broadcasted_iota(jnp.int32, (TOK, SLOTS), 0)
    slot_iota = lax.broadcasted_iota(jnp.int32, (1, SLOTS), 1)
    own_row = index_ref[pl.ds(z, 1), :]
    pick = (tok_iota == own_row).astype(F32).astype(BF16)
    picked = dot(pick, hidden_ref[0], ((0,), (0,))).astype(BF16)
    for p in (0, 1):
        zrow[p, z] = picked[:, HF * p : HF * (p + 1)]
    tea = teacher_ref[...].astype(F32).T
    top = jnp.max(tea, axis=0, keepdims=True)
    zt[z, 0:1] = top
    zt[z, 1:2] = jnp.sum(jnp.exp(tea - top), axis=0, keepdims=True)
    for s in range(NZ):
        live_row = jnp.where(slot_iota < count_ref[s], index_ref[s : s + 1, :], -1)
        hot[s] = (tok_iota == live_row).astype(F32).astype(BF16)
    pl.semaphore_wait(barrier, len(partners))
    for p in (0, 1):
        for d in PEERS_Z:
            send("z%d" % p, "z%d" % p, zrow.at[p, z], zrow.at[p, z], to_z(d))
    for d in PEERS_Z:
        send("zt", "zt", zt.at[z], zt.at[z], to_z(d))

    def off(p, d1, d2):
        return (d1, d2) if p == 0 else (d2, d1)

    def axis1(p, d):
        return to_xy(d, 0) if p == 0 else to_xy(0, d)

    def axis2(p, d):
        return to_xy(0, d) if p == 0 else to_xy(d, 0)

    def block(p, o, h=None, core=None):
        at = vid(*o, c if core is None else core)
        if h is None:
            return rows.at[at, p]
        return rows.at[at, p, pl.ds(HT * h, HT)]

    def relay(p, o):
        send("cg", ("core", o), block(p, o), block(p, o), sibling)

    sides = ((0, -1, 1), (1, 1, -1))

    def spread(p, d, o, axis):
        if d not in RING_G:
            send("g", ("ring", p, d, 2), block(p, o), block(p, o), axis(p, 2))
        send("g", ("ring", p, d, 0), block(p, o), block(p, o), axis(p, 1))
        send("g", ("ring", p, d, 1), block(p, o), block(p, o), axis(p, -1))

    def forward(p, d, o, s, axis):
        if d in RING_G:
            send("g", ("ring", p, d, 2), block(p, o, s), block(p, o, s), axis(p, sides[s][2]))

    squares = None
    for p in (0, 1):
        got("z%d" % p, zrow.at[p, pl.ds(0, NZ - 1)])
        mine = dot(hot[0], zrow[p, 0], ((1,), (0,)))
        for s in range(1, NZ):
            mine = mine + dot(hot[s], zrow[p, s], ((1,), (0,)))
        rows[v, p] = mine.astype(BF16)
        spread(p, "one", (0, 0), axis1)
        spread(p, 0, (0, 0), axis2)
        relay(p, (0, 0))
        squares = mine * mine if p == 0 else squares + mine * mine
    squares = squares.T

    def merge(buf, n, at):
        m = buf[0, at : at + 1]
        for i in range(1, n):
            m = jnp.maximum(m, buf[i, at : at + 1])
        t = jnp.zeros_like(m)
        for i in range(n):
            t = t + buf[i, at + 1 : at + 2] * jnp.exp(buf[i, at : at + 1] - m)
        return m, t

    def total(buf, n, at):
        t = buf[0, at : at + 1]
        for i in range(1, n):
            t = t + buf[i, at : at + 1]
        return t

    got("zt", zt.at[pl.ds(0, NZ - 1)])
    q_me = qid(0, 0)
    m, t = merge(zt, NZ, 0)
    xt[q_me, 0:1] = m
    xt[q_me, 1:2] = t
    xt[q_me, 2:3] = jnp.sum(squares, axis=0, keepdims=True)
    for o in PEERS_XY:
        send("xt", "xt", xt.at[q_me], xt.at[q_me], to_xy(*o))

    have = {(0, 0): 2}
    ready = []

    def arrived(p, o):
        relay(p, o)
        have[o] = have.get(o, 0) + 1
        if have[o] == 2:
            ready.append((o, c))

    for p in (0, 1):
        for s, frm, to in sides:
            o = off(p, frm, 0)
            got(("ring", p, "one", s), block(p, o))
            forward(p, "one", o, s, axis1)
            spread(p, frm, o, axis2)
            arrived(p, o)

    got("xt", xt.at[pl.ds(0, NX * NY - 1)])
    m, t = merge(xt, NX * NY, 0)
    ct[c, 0:1] = m
    ct[c, 1:2] = t
    ct[c, 2:3] = total(xt, NX * NY, 2)
    send("ct", "ct", ct.at[c], ct.at[c], sibling)
    for p in (0, 1):
        o = off(p, 2, 0)
        got(("ring", p, "one", 2), block(p, o))
        spread(p, 2, o, axis2)
        arrived(p, o)

    stu[...] = jnp.zeros_like(stu)
    for cp in loads:
        cp.wait()
    got("ct", ct.at[c])
    m, t = merge(ct, NC, 0)
    lse_t = m + jnp.log(t)
    inv = lax.rsqrt(total(ct, NC, 2) / (NV * FC) + EPS)
    inv_col = jnp.broadcast_to(inv, (HF, TOK)).T
    inv_wide = jnp.concatenate([inv_col, inv_col], axis=1)

    def score(chunk):
        raw = jnp.concatenate([rows[chunk, 0], rows[chunk, 1]], axis=1)
        normed = (raw.astype(F32) * inv_wide * gain(chunk)).astype(BF16)
        stu[...] += dot(normed, head[chunk], ((1,), (0,)))

    def score_sibling(o):
        got(("core", o), rows.at[vid(*o, other)])
        score(vid(*o, other))

    scored = []

    def drain(lag):
        while ready:
            o, _ = ready.pop(0)
            score(vid(*o, c))
            scored.append(o)
        while len(scored) > lag:
            score_sibling(scored.pop(0))

    ready.insert(0, ((0, 0), c))
    for d in (0, 1, -1):
        for p in (0, 1):
            for s, frm, to in sides:
                o = off(p, d, frm)
                got(("ring", p, d, s), block(p, o))
                forward(p, d, o, s, axis2)
                arrived(p, o)
        drain(4)
    prob = jnp.exp(tea - lse_t)
    weight = (layer_ref[...].astype(F32) + 1.0) / LAYERS
    for d in (0, 2, 1, -1):
        for p in (0, 1):
            if d == 2:
                for s, frm, to in sides:
                    o = off(p, d, frm)
                    got(("ring", p, d, s), block(p, o))
                    forward(p, d, o, s, axis2)
                    arrived(p, o)
            o = off(p, d, 2)
            got(("ring", p, d, 2), block(p, o))
            arrived(p, o)
        drain(3)
    drain(0)
    student = stu[...].T
    m = jnp.max(student, axis=0, keepdims=True)
    cs[c, 0:1] = m
    cs[c, 1:2] = jnp.sum(jnp.exp(student - m), axis=0, keepdims=True)
    cs[c, 2:3] = jnp.sum(prob * (tea - student), axis=0, keepdims=True)
    send("cs", "cs", cs.at[c], cs.at[c], sibling)
    got("cs", cs.at[c])
    m, t = merge(cs, NC, 0)
    zs[z, 0:1] = m
    zs[z, 1:2] = t
    zs[z, 2:3] = total(cs, NC, 2)
    for d in PEERS_Z:
        send("zs", "zs", zs.at[z], zs.at[z], to_z(d))
    got("zs", zs.at[pl.ds(0, NZ - 1)])
    m, t = merge(zs, NZ, 0)
    xs[q_me, 0:1] = m
    xs[q_me, 1:2] = t
    xs[q_me, 2:3] = total(zs, NZ, 2)
    for o in PEERS_XY:
        send("xs", "xs", xs.at[q_me], xs.at[q_me], to_xy(*o))
    got("xs", xs.at[pl.ds(0, NX * NY - 1)])
    m, t = merge(xs, NX * NY, 0)
    lse_s = m + jnp.log(t)
    kl = total(xs, NX * NY, 2) - lse_t + lse_s
    dlogit = (weight * (jnp.exp(student - lse_s) - prob)).T.astype(BF16)
    def part(chunk):
        return dot(dlogit, head[chunk], ((1,), (1,)))

    def own(o):
        return PLANE.index(o)

    def slot(d):
        return OFFS.index(d) if d != "one" else 4

    def chunk_at(p, d, d1):
        return own(off(p, d1, 0)) if d == "one" else own(off(p, d, d1))

    def give(p, d, d1, axis):
        i, k = chunk_at(p, d, d1), slot(d)
        if d not in RING_R:
            j = (1, -1, 2).index(d1)
            full_out[p, k, j] = part_sum[i, p].astype(BF16)
            send("r", ("ring", p, d, 2), full_out.at[p, k, j], full_in.at[p, k, j], axis(p, d1))
        elif d1 == 2:
            for h in (0, 1):
                half_out[p, k, h] = part_sum[i, p, pl.ds(HT * h, HT)].astype(BF16)
                send("r", ("ring", p, d, h), half_out.at[p, k, h], half_in.at[p, k, h], axis(p, 1 - 2 * h))

    def pass_on(p, d, axis):
        if d not in RING_R:
            return
        k = slot(d)
        for s in (0, 1):
            i = chunk_at(p, d, 1 - 2 * s)
            got(("ring", p, d, s), half_in.at[p, k, s])
            near = pl.ds(HT * s, HT)
            rest = pl.ds(HT * (1 - s), HT)
            full_out[p, k, s, near] = (part_sum[i, p, near] + half_in[p, k, s].astype(F32)).astype(BF16)
            full_out[p, k, s, rest] = part_sum[i, p, rest].astype(BF16)
            send("r", ("ring", p, d, 2), full_out.at[p, k, s], full_in.at[p, k, s], axis(p, 1 - 2 * s))

    def collect(p, d):
        i, k = chunk_at(p, d, 0), slot(d)
        n = 2 if d in RING_R else 3
        got(("ring", p, d, 2), full_in.at[p, k, pl.ds(0, n)])
        value = part_sum[i, p]
        for j in range(n):
            value = value + full_in[p, k, j].astype(F32)
        return value

    def settle(o):
        i = own(o)
        got(("core", o), cross_in.at[i])
        for p in (0, 1):
            part_sum[i, p] = part_sum[i, p] + cross_in[i, p].astype(F32)
            d1, d2 = o[::-1] if p == 0 else o
            if d1 != 0:
                give(p, d2, d1, axis2)

    lag = 3
    for k, o in enumerate(FAR):
        i = own(o)
        value = part(vid(*o, other)).astype(BF16)
        for p in (0, 1):
            cross_out[i, p] = value[:, HF * p : HF * (p + 1)]
        send("cr2", ("core", o), cross_out.at[i], cross_in.at[i], sibling)
        value = part(vid(*o, c))
        for p in (0, 1):
            part_sum[i, p] = value[:, HF * p : HF * (p + 1)]
        if k >= lag:
            settle(FAR[k - lag])
    for o in FAR[-lag:]:
        settle(o)

    for p in (0, 1):
        pass_on(p, 2, axis2)
    for p in (0, 1):
        pass_on(p, 1, axis2)
        pass_on(p, -1, axis2)
    for d in (2, 1, -1):
        for p in (0, 1):
            part_sum[chunk_at(p, d, 0), p] = collect(p, d)
            give(p, "one", d, axis1)
        if d == 2:
            for p in (0, 1):
                pass_on(p, 0, axis2)
    for p in (0, 1):
        pass_on(p, "one", axis1)
    for p in (0, 1):
        part_sum[own((0, 0)), p] = collect(p, 0)

    hot_own = hot[z]
    two = lax.broadcasted_iota(jnp.int32, (16, SLOTS), 0) + 2 * v == lax.broadcasted_iota(jnp.int32, (16, SLOTS), 1)
    sel_f = dot(two.astype(F32).astype(BF16), hot_own, ((1,), (1,)))
    sel = sel_f.astype(BF16)
    inv_two = jnp.sum(sel_f[0:2] * inv, axis=1, keepdims=True)
    for i in range(NV):
        for p in (0, 1):
            unit_ref[:, pl.ds(FC * i + HF * p, HF)] = dot(sel, rows[i, p], ((1,), (0,)))[0:2] * inv_two
    kl_col = jnp.broadcast_to(kl, (HF, TOK)).T
    out_ref[0:1, NV * FC : NV * FC + SLOTS] = jnp.sum(hot_own.astype(F32) * kl_col[:, :SLOTS], axis=0, keepdims=True)
    out_ref[1:2, NV * FC : NV * FC + 1] = jnp.sum(weight * kl, axis=1, keepdims=True) / TOK

    mine = []
    for p in (0, 1):
        whole = collect(p, "one").astype(BF16)
        for k, d in enumerate(PEERS_Z):
            z_out[p, k] = dot(hot[zid(d)], whole, ((0,), (0,))).astype(BF16)
            send("zg%d" % p, "zg%d" % p, z_out.at[p, k], z_in.at[p, k], to_z(d))
        mine.append(dot(hot_own, whole, ((0,), (0,))))
    grads = []
    for p in (0, 1):
        got("zg%d" % p, z_in.at[p])
        value = mine[p]
        for k in range(NZ - 1):
            value = value + z_in[p, k].astype(F32)
        grads.append(value)
    grads = jnp.concatenate(grads, axis=1)
    for q in range(NX * NY):
        for cc in range(NC):
            j = (q * NC + cc) * 2
            tr_out[q, cc] = grads[j : j + 2]
    for k, o in enumerate(PEERS_XY):
        send("tr", "tr", tr_out.at[qid(*o)], tr_in.at[q_me], to_xy(*o))
    tr_in[q_me] = tr_out[q_me]
    got("tr", tr_in.at[pl.ds(0, NX * NY - 1)])
    send("cr", "cr", tr_in.at[:, other], tr_side, sibling)
    got("cr", tr_side)
    both = []
    acc = jnp.zeros((2, FC), F32)
    for q in range(NX * NY):
        for cc in range(NC):
            i = q * NC + cc
            dn = jnp.where(c == cc, tr_in[q, cc], tr_side[q]) * gain(i)
            both.append(dn)
            acc = acc + dn * unit_ref[:, FC * i : FC * (i + 1)]
    mean = jnp.sum(acc, axis=1, keepdims=True) / (NV * FC)
    for i in range(NV):
        at = slice(FC * i, FC * (i + 1))
        out_ref[:, at] = inv_two * (both[i] - unit_ref[:, at] * mean)
    for k in ("z0", "z1"):
        sent(k, zrow.at[0, pl.ds(0, NZ - 1)])
    for k in ("zt", "zs"):
        sent(k, zt.at[pl.ds(0, NZ - 1)])
    for k in ("xt", "xs"):
        sent(k, xt.at[pl.ds(0, NX * NY - 1)])
    for k in ("ct", "cs"):
        sent(k, ct.at[c])
    for k in ("g", "r"):
        sent(k, rows.at[pl.ds(0, 15)])
    for k in ("cg", "cr2"):
        sent(k, rows.at[pl.ds(0, 16)])
    for k in ("zg0", "zg1"):
        sent(k, z_out.at[0])
    sent("tr", tr_out.at[pl.ds(0, NX * NY - 1)])
    sent("cr", tr_side)


def on_device(section_hidden, norm_gain, head, teacher_logits, exit_layer, row_count, row_index):
    packed = pl.pallas_call(
        kernel,
        out_shape=pltpu.VMEM((2, NV * FC + 128), F32),
        in_specs=[pl.BlockSpec(memory_space=pltpu.HBM)] * 7,
        out_specs=pl.BlockSpec(memory_space=pltpu.VMEM),
        scratch_shapes=[
            pltpu.VMEM((1, TOK, FC), BF16),
            pltpu.VMEM((2 * NV, 128), F32),
            pltpu.VMEM((TOK, FC), BF16),
            pltpu.VMEM((1, TOK), jnp.int32),
            pltpu.SMEM((NZ,), jnp.int32),
            pltpu.VMEM((NZ, SLOTS), jnp.int32),
            pltpu.VMEM((NV, FC, TOK), BF16),
            pltpu.VMEM((NV, 2, TOK, HF), BF16),
            pltpu.VMEM((2, NZ, SLOTS, HF), BF16),
            pltpu.VMEM((NZ, 4, TOK), F32),
            pltpu.VMEM((NZ, 4, TOK), F32),
            pltpu.VMEM((NX * NY, 4, TOK), F32),
            pltpu.VMEM((NX * NY, 4, TOK), F32),
            pltpu.VMEM((NC, 4, TOK), F32),
            pltpu.VMEM((NC, 4, TOK), F32),
            pltpu.VMEM((NZ, TOK, SLOTS), BF16),
            pltpu.VMEM((16, 2, TOK, HF), BF16),
            pltpu.VMEM((16, 2, TOK, HF), BF16),
            pltpu.VMEM((16, 2, TOK, HF), F32),
            pltpu.VMEM((2, 5, 2, HT, HF), BF16),
            pltpu.VMEM((2, 5, 2, HT, HF), BF16),
            pltpu.VMEM((2, 5, 3, TOK, HF), BF16),
            pltpu.VMEM((2, 5, 3, TOK, HF), BF16),
            pltpu.VMEM((2, NZ - 1, SLOTS, HF), BF16),
            pltpu.VMEM((2, NZ - 1, SLOTS, HF), BF16),
            pltpu.VMEM((16, 2, 2, FC), F32),
            pltpu.VMEM((16, 2, 2, FC), F32),
            pltpu.VMEM((16, 2, FC), F32),
            pltpu.VMEM((2, NV * FC), F32),
            pltpu.VMEM((TOK, 256), F32),
            pltpu.SemaphoreType.DMA((6,)),
            pltpu.SemaphoreType.DMA((4,)),
            pltpu.SemaphoreType.DMA((len(GROUPS),)),
            pltpu.SemaphoreType.DMA((len(NAMES),)),
        ],
        compiler_params=pltpu.CompilerParams(collective_id=0, has_side_effects=True, vmem_limit_bytes=60 * 2**20),
        name="exit_loss",
    )(
        section_hidden,
        norm_gain.reshape(2 * NV, 128),
        head.reshape(NV, FC, head.shape[1]),
        teacher_logits,
        exit_layer.reshape(1, TOK),
        row_count,
        row_index,
    )
    wide = NV * FC
    return packed[0:1, wide : wide + SLOTS], packed[1, wide], packed[None, :, :wide].astype(BF16)


def solution(mesh):
    return jax.shard_map(
        on_device,
        mesh=mesh,
        in_specs=(
            P("section", None, "vocab"),
            P(),
            P(None, ("section", "vocab")),
            P(None, ("section", "vocab")),
            P(),
            P(),
            P(),
        ),
        out_specs=(P("section", None), P(), P("section", "vocab", None)),
        check_vma=False,
    )
```

time: 635 us -> 81.6 us (0.13)
  waiting for transfers between devices: 417 us -> 0 us
  blocking collectives: 149 us -> 0 us
  Pallas kernels: 0 us -> 79.2 us
  other arithmetic: 24.1 us -> 0 us
  matrix products: 18 us -> 0 us
  between operations: 15.6 us -> 0.64 us
  local copies, waits for them, and re-layouts: 9.6 us -> 1.66 us
    unnamed x4 -> x0, waiting for transfers between devices: 278 us -> none
    all_gather x2 -> x0, waiting for transfers between devices: 139 us -> none  [the longest x1 86.7 us: on_device(): all_rows = lax.all_gather(wide_rows, 'section', axis=0, tiled=True)]
    pallas_call x0 -> x1, Pallas kernels: none -> 79.2 us  [on_device(): pl.pallas_call(kernel, out_shape=pltpu.VMEM((2, NV * FC + 128), F32), in_...]
    pmax x1 -> x0, blocking collectives: 76.4 us -> none  [on_device(): lax.pmax((teacher_local, student_local), ('section', 'vocab'))]
    psum x1 -> x0, blocking collectives: 72.8 us -> none  [on_device(): lax.psum((jnp.sum(teacher_exp, axis=1), jnp.sum(teacher_exp * (teacher -...]
    dot_general x2 -> x0, matrix products: 18 us -> none  [the longest x1 10.4 us: on_device(): lax.dot_general(dlogit, head, (((1,), (1,)), ((), ())), preferred_element...]
    mul x1 -> x0, other arithmetic: 12.2 us -> none  [on_device(): unit_rows = rows_f32 * inv_rms]
    gather x4 -> x0, local copies, waits for them, and re-layouts: 7.3 us -> none  [the longest x1 3.62 us: on_device(): jnp.take(exit_layer, row_tokens).astype(jnp.float32) + 1.0]
  transfers between devices with their start and end apart: 3 -> 0, of which waited for: 3 -> 0; matrix products, arithmetic and copies ran while one was open for 3% -> 0% of each run, Pallas kernels for 0% -> 0%
where the time goes in v2:
time: 81.6 us; the launch traced here: 81.5 us
  Pallas kernels  79.2 us (97%)
  local copies, waits for them, and re-layouts  1.66 us (2%)
    pallas_call x1, Pallas kernels, on_device(): pl.pallas_call(kernel, out_shape=pltpu.VMEM((2, NV * FC + 128), F32), in_...  79.2 us

profile of v2, /device:TPU:1, one launch (start us, length us, event | category | flops | bytes accessed | tf_op | source)
XLA Modules:
  0.0 81.5 jit_solution(12013091292665703809)
XLA Ops:
  0.6 79.2 %exit_loss.1 = f32[2,8320]{1,0:T(2,128)S(1)} custom-call(bf16[1,256,256]{2,1,0:T(8,128)(2,1)} %hidden_hbm.1, f32[64,128]{1,0:T(8,128)} %bitcast.7, bf16[32,256,256]{2,1,0:T(8,128)(2,1)} %bitcast.6, bf16[256,256]{1,0:T(8,128)(2,1)} %teacher_hbm.1, s32[1,256]{1,0:T(1,128)} %bitcast.8, s32[8]{0:T(128)} %count_hbm.1, s32[8,64]{1,0:T(8,128)} %index_hbm.1), custom_call_target="tpu_custom_call" | custom-call | tf_op jit(solution)/shard_map/exit_loss/pallas_call | solution.py:453
  79.8 0.5 slice.11
  80.4 0.5 slice.10
  80.9 0.6 fusion

commit v3 on v2

--- a/solution.py
+++ b/solution.py
@@ -22,22 +22,23 @@
 PLANE = [(a, b) for a in OFFS for b in OFFS]
 PEERS_XY = sorted((o for o in PLANE if o != (0, 0)), key=lambda o: -abs(o[0]) - abs(o[1]))
 PEERS_Z = (4, 3, -3, 2, -2, 1, -1)
+NP = NZ * NC
 FAR = [(2, 2), (2, 1), (1, 2), (2, -1), (-1, 2), (2, 0), (0, 2), (1, 1), (-1, 1), (1, -1), (-1, -1), (0, 1), (1, 0), (0, -1), (-1, 0), (0, 0)]
 
 
 RING_G = (0, 1, -1)
-RING_R = (0, 1, -1)
+RING_R = (0,)
 
 
 def all_names():
-    names = ["z0", "z1", "zt", "xt", "ct", "cs", "zs", "xs", "zg0", "zg1", "tr", "cr"]
+    names = ["z0", "z1", "zt", "xt", "zs", "xs", "zg0", "zg1", "tr"]
     names += [("ring", p, d, k) for p in (0, 1) for d in OFFS + ("one",) for k in range(3)]
     names += [("core", o) for o in PLANE]
     return {k: i for i, k in enumerate(names)}
 
 
 NAMES = all_names()
-GROUPS = {k: i for i, k in enumerate(["z0", "z1", "zt", "xt", "ct", "cs", "zs", "xs", "zg0", "zg1", "tr", "cr", "g", "r", "cg", "cr2"])}
+GROUPS = {k: i for i, k in enumerate(["z0", "z1", "zt", "xt", "zs", "xs", "zg0", "zg1", "tr", "g", "r", "cg", "cr2"])}
 
 
 def dot(a, b, dims):
@@ -48,9 +49,9 @@
     hidden_hbm, gain_hbm, head_hbm, teacher_hbm, layer_hbm, count_hbm, index_hbm,
     out_ref,
     hidden_ref, gain_ref, teacher_ref, layer_ref, count_ref, index_ref, head,
-    rows, zrow, zt, zs, xt, xs, ct, cs,
-    hot, cross_out, cross_in, part_sum, half_out, half_in, full_out, full_in,
-    z_out, z_in, tr_out, tr_in, tr_side, unit_ref,
+    rows, zrow, zt, zs, xt, xs,
+    hot, hot_all, hot_t, cross_out, cross_in, part_sum, half_out, half_in, full_out, full_in,
+    z_out, z_in, tr_out, tr_in, unit_ref,
     stu, load_sem, head_sem, send_sem, recv_sem,
 ):
     z = lax.axis_index("section")
@@ -73,7 +74,15 @@
     def to_z(dz):
         return (zid(dz), v)
 
+    def column(dz, core):
+        return (zid(dz), vid(0, 0, core))
+
     sibling = (z, vid(0, 0, other))
+    pairs = [(d, k) for d in PEERS_Z for k in (0, 1)] + [(0, 1)]
+    me = z * NC + c
+
+    def to_pair(d, k):
+        return column(d, c if k == 0 else other)
 
     def send(group, name, src, dst, target):
         pltpu.make_async_remote_copy(
@@ -90,7 +99,7 @@
         return jnp.concatenate([gain_ref[pl.ds(2 * chunk, 1), :], gain_ref[pl.ds(2 * chunk + 1, 1), :]], axis=1)
 
     barrier = pltpu.get_barrier_semaphore()
-    partners = [to_z(d) for d in PEERS_Z] + [to_xy(*o) for o in PEERS_XY] + [sibling]
+    partners = [to_pair(*o) for o in pairs] + [to_xy(*o) for o in PEERS_XY]
     for t in partners:
         pl.semaphore_signal(barrier, inc=1, device_id=t, device_id_type=MESH)
     small = [(index_hbm, index_ref), (hidden_hbm, hidden_ref), (teacher_hbm, teacher_ref), (count_hbm, count_ref), (gain_hbm, gain_ref), (layer_hbm, layer_ref)]
@@ -108,19 +117,32 @@
     picked = dot(pick, hidden_ref[0], ((0,), (0,))).astype(BF16)
     for p in (0, 1):
         zrow[p, z] = picked[:, HF * p : HF * (p + 1)]
+    squares = picked.astype(F32)
+    squares = squares * squares
+    squares = (squares[:, :HF] + squares[:, HF:]).T
+    q_me = qid(0, 0)
     tea = teacher_ref[...].astype(F32).T
     top = jnp.max(tea, axis=0, keepdims=True)
-    zt[z, 0:1] = top
-    zt[z, 1:2] = jnp.sum(jnp.exp(tea - top), axis=0, keepdims=True)
+    xt[q_me, 0:1] = top
+    xt[q_me, 1:2] = jnp.sum(jnp.exp(tea - top), axis=0, keepdims=True)
+    xt[q_me, 2:3, 0:SLOTS] = jnp.sum(squares, axis=0, keepdims=True)
     for s in range(NZ):
         live_row = jnp.where(slot_iota < count_ref[s], index_ref[s : s + 1, :], -1)
         hot[s] = (tok_iota == live_row).astype(F32).astype(BF16)
+        hot_all[:, SLOTS * s : SLOTS * (s + 1)] = hot[s]
     pl.semaphore_wait(barrier, len(partners))
-    for p in (0, 1):
-        for d in PEERS_Z:
-            send("z%d" % p, "z%d" % p, zrow.at[p, z], zrow.at[p, z], to_z(d))
     for d in PEERS_Z:
-        send("zt", "zt", zt.at[z], zt.at[z], to_z(d))
+        send("z0", "z0", zrow.at[0, z], zrow.at[0, z], to_z(d))
+    for o in PEERS_XY:
+        send("xt", "xt", xt.at[q_me], xt.at[q_me], to_xy(*o))
+    for d in PEERS_Z:
+        send("z1", "z1", zrow.at[1, z], zrow.at[1, z], to_z(d))
+
+    row = lax.broadcasted_iota(jnp.int32, (SLOTS, SLOTS), 0)
+    col = lax.broadcasted_iota(jnp.int32, (SLOTS, SLOTS), 1)
+    perm = (row == 4 * ((col % 32) // 2) + 2 * (col // 32) + col % 2).astype(F32).astype(BF16)
+    for s in range(NZ):
+        hot_t[s] = dot(hot[s], perm, ((1,), (0,))).T.astype(BF16)
 
     def off(p, d1, d2):
         return (d1, d2) if p == 0 else (d2, d1)
@@ -143,27 +165,14 @@
     sides = ((0, -1, 1), (1, 1, -1))
 
     def spread(p, d, o, axis):
+        send("g", ("ring", p, d, 0), block(p, o), block(p, o), axis(p, 1))
+        send("g", ("ring", p, d, 1), block(p, o), block(p, o), axis(p, -1))
         if d not in RING_G:
             send("g", ("ring", p, d, 2), block(p, o), block(p, o), axis(p, 2))
-        send("g", ("ring", p, d, 0), block(p, o), block(p, o), axis(p, 1))
-        send("g", ("ring", p, d, 1), block(p, o), block(p, o), axis(p, -1))
 
     def forward(p, d, o, s, axis):
         if d in RING_G:
             send("g", ("ring", p, d, 2), block(p, o, s), block(p, o, s), axis(p, sides[s][2]))
-
-    squares = None
-    for p in (0, 1):
-        got("z%d" % p, zrow.at[p, pl.ds(0, NZ - 1)])
-        mine = dot(hot[0], zrow[p, 0], ((1,), (0,)))
-        for s in range(1, NZ):
-            mine = mine + dot(hot[s], zrow[p, s], ((1,), (0,)))
-        rows[v, p] = mine.astype(BF16)
-        spread(p, "one", (0, 0), axis1)
-        spread(p, 0, (0, 0), axis2)
-        relay(p, (0, 0))
-        squares = mine * mine if p == 0 else squares + mine * mine
-    squares = squares.T
 
     def merge(buf, n, at):
         m = buf[0, at : at + 1]
@@ -180,15 +189,6 @@
             t = t + buf[i, at : at + 1]
         return t
 
-    got("zt", zt.at[pl.ds(0, NZ - 1)])
-    q_me = qid(0, 0)
-    m, t = merge(zt, NZ, 0)
-    xt[q_me, 0:1] = m
-    xt[q_me, 1:2] = t
-    xt[q_me, 2:3] = jnp.sum(squares, axis=0, keepdims=True)
-    for o in PEERS_XY:
-        send("xt", "xt", xt.at[q_me], xt.at[q_me], to_xy(*o))
-
     have = {(0, 0): 2}
     ready = []
 
@@ -198,35 +198,56 @@
         if have[o] == 2:
             ready.append((o, c))
 
-    for p in (0, 1):
+    def start(p):
+        got("z%d" % p, zrow.at[p, pl.ds(0, NZ - 1)])
+        mine = dot(hot_all[...], zrow[p].reshape(NZ * SLOTS, HF), ((1,), (0,)))
+        rows[v, p] = mine.astype(BF16)
+        spread(p, "one", (0, 0), axis1)
+        spread(p, 0, (0, 0), axis2)
+        relay(p, (0, 0))
+
+    def first(p):
         for s, frm, to in sides:
             o = off(p, frm, 0)
             got(("ring", p, "one", s), block(p, o))
             forward(p, "one", o, s, axis1)
             spread(p, frm, o, axis2)
             arrived(p, o)
-
-    got("xt", xt.at[pl.ds(0, NX * NY - 1)])
-    m, t = merge(xt, NX * NY, 0)
-    ct[c, 0:1] = m
-    ct[c, 1:2] = t
-    ct[c, 2:3] = total(xt, NX * NY, 2)
-    send("ct", "ct", ct.at[c], ct.at[c], sibling)
-    for p in (0, 1):
+        for s, frm, to in sides:
+            o = off(p, 0, frm)
+            got(("ring", p, 0, s), block(p, o))
+            forward(p, 0, o, s, axis2)
+            arrived(p, o)
         o = off(p, 2, 0)
         got(("ring", p, "one", 2), block(p, o))
         spread(p, 2, o, axis2)
         arrived(p, o)
 
+    start(0)
+    got("xt", xt.at[pl.ds(0, NX * NY - 1)])
+    m, t = merge(xt, NX * NY, 0)
+    zt[me, 0:1] = m
+    zt[me, 1:2] = t
+    zt[me, 2:3] = total(xt, NX * NY, 2)
+    for o in pairs:
+        send("zt", "zt", zt.at[me], zt.at[me], to_pair(*o))
+    start(1)
+    first(0)
+    first(1)
     stu[...] = jnp.zeros_like(stu)
     for cp in loads:
         cp.wait()
-    got("ct", ct.at[c])
-    m, t = merge(ct, NC, 0)
+    got("zt", zt.at[pl.ds(0, NP - 1)])
+    m, t = merge(zt, NP, 0)
     lse_t = m + jnp.log(t)
-    inv = lax.rsqrt(total(ct, NC, 2) / (NV * FC) + EPS)
-    inv_col = jnp.broadcast_to(inv, (HF, TOK)).T
-    inv_wide = jnp.concatenate([inv_col, inv_col], axis=1)
+    spots = jnp.zeros((TOK, SLOTS), F32)
+
+    def inverse(s):
+        return lax.rsqrt((zt[NC * s, 2:3, 0:SLOTS] + zt[NC * s + 1, 2:3, 0:SLOTS]) / (NV * FC) + EPS)
+
+    for s in range(NZ):
+        spots = spots + hot[s].astype(F32) * inverse(s)
+    inv_wide = jnp.broadcast_to(jnp.sum(spots, axis=1, keepdims=True), (TOK, FC))
 
     def score(chunk):
         raw = jnp.concatenate([rows[chunk, 0], rows[chunk, 1]], axis=1)
@@ -248,7 +269,8 @@
             score_sibling(scored.pop(0))
 
     ready.insert(0, ((0, 0), c))
-    for d in (0, 1, -1):
+    drain(4)
+    for d in (1, -1):
         for p in (0, 1):
             for s, frm, to in sides:
                 o = off(p, d, frm)
@@ -273,22 +295,16 @@
     drain(0)
     student = stu[...].T
     m = jnp.max(student, axis=0, keepdims=True)
-    cs[c, 0:1] = m
-    cs[c, 1:2] = jnp.sum(jnp.exp(student - m), axis=0, keepdims=True)
-    cs[c, 2:3] = jnp.sum(prob * (tea - student), axis=0, keepdims=True)
-    send("cs", "cs", cs.at[c], cs.at[c], sibling)
-    got("cs", cs.at[c])
-    m, t = merge(cs, NC, 0)
-    zs[z, 0:1] = m
-    zs[z, 1:2] = t
-    zs[z, 2:3] = total(cs, NC, 2)
-    for d in PEERS_Z:
-        send("zs", "zs", zs.at[z], zs.at[z], to_z(d))
-    got("zs", zs.at[pl.ds(0, NZ - 1)])
-    m, t = merge(zs, NZ, 0)
+    zs[me, 0:1] = m
+    zs[me, 1:2] = jnp.sum(jnp.exp(student - m), axis=0, keepdims=True)
+    zs[me, 2:3] = jnp.sum(prob * (tea - student), axis=0, keepdims=True)
+    for o in pairs:
+        send("zs", "zs", zs.at[me], zs.at[me], to_pair(*o))
+    got("zs", zs.at[pl.ds(0, NP - 1)])
+    m, t = merge(zs, NP, 0)
     xs[q_me, 0:1] = m
     xs[q_me, 1:2] = t
-    xs[q_me, 2:3] = total(zs, NZ, 2)
+    xs[q_me, 2:3] = total(zs, NP, 2)
     for o in PEERS_XY:
         send("xs", "xs", xs.at[q_me], xs.at[q_me], to_xy(*o))
     got("xs", xs.at[pl.ds(0, NX * NY - 1)])
@@ -308,16 +324,18 @@
     def chunk_at(p, d, d1):
         return own(off(p, d1, 0)) if d == "one" else own(off(p, d, d1))
 
-    def give(p, d, d1, axis):
+    def give(p, d, d1, axis, value):
         i, k = chunk_at(p, d, d1), slot(d)
-        if d not in RING_R:
+        if d1 != 0 and d not in RING_R:
             j = (1, -1, 2).index(d1)
-            full_out[p, k, j] = part_sum[i, p].astype(BF16)
+            full_out[p, k, j] = value.astype(BF16)
             send("r", ("ring", p, d, 2), full_out.at[p, k, j], full_in.at[p, k, j], axis(p, d1))
         elif d1 == 2:
             for h in (0, 1):
-                half_out[p, k, h] = part_sum[i, p, pl.ds(HT * h, HT)].astype(BF16)
+                half_out[p, k, h] = value[HT * h : HT * (h + 1)].astype(BF16)
                 send("r", ("ring", p, d, h), half_out.at[p, k, h], half_in.at[p, k, h], axis(p, 1 - 2 * h))
+        else:
+            part_sum[i, p] = value
 
     def pass_on(p, d, axis):
         if d not in RING_R:
@@ -343,40 +361,34 @@
 
     def settle(o):
         i = own(o)
+        value = part(vid(*o, c))
         got(("core", o), cross_in.at[i])
         for p in (0, 1):
-            part_sum[i, p] = part_sum[i, p] + cross_in[i, p].astype(F32)
             d1, d2 = o[::-1] if p == 0 else o
-            if d1 != 0:
-                give(p, d2, d1, axis2)
+            give(p, d2, d1, axis2, value[:, HF * p : HF * (p + 1)] + cross_in[i, p].astype(F32))
 
     lag = 3
     for k, o in enumerate(FAR):
-        i = own(o)
         value = part(vid(*o, other)).astype(BF16)
         for p in (0, 1):
-            cross_out[i, p] = value[:, HF * p : HF * (p + 1)]
-        send("cr2", ("core", o), cross_out.at[i], cross_in.at[i], sibling)
-        value = part(vid(*o, c))
-        for p in (0, 1):
-            part_sum[i, p] = value[:, HF * p : HF * (p + 1)]
+            cross_out[own(o), p] = value[:, HF * p : HF * (p + 1)]
+        send("cr2", ("core", o), cross_out.at[own(o)], cross_in.at[own(o)], sibling)
         if k >= lag:
             settle(FAR[k - lag])
     for o in FAR[-lag:]:
         settle(o)
 
+    for d in (2, 1, -1):
+        for p in (0, 1):
+            pass_on(p, d, axis2)
+        for p in (0, 1):
+            if d == 2:
+                give(p, "one", d, axis1, collect(p, d))
     for p in (0, 1):
-        pass_on(p, 2, axis2)
-    for p in (0, 1):
-        pass_on(p, 1, axis2)
-        pass_on(p, -1, axis2)
-    for d in (2, 1, -1):
-        for p in (0, 1):
-            part_sum[chunk_at(p, d, 0), p] = collect(p, d)
-            give(p, "one", d, axis1)
-        if d == 2:
-            for p in (0, 1):
-                pass_on(p, 0, axis2)
+        pass_on(p, 0, axis2)
+    for d in (1, -1):
+        for p in (0, 1):
+            give(p, "one", d, axis1, collect(p, d))
     for p in (0, 1):
         pass_on(p, "one", axis1)
     for p in (0, 1):
@@ -386,7 +398,8 @@
     two = lax.broadcasted_iota(jnp.int32, (16, SLOTS), 0) + 2 * v == lax.broadcasted_iota(jnp.int32, (16, SLOTS), 1)
     sel_f = dot(two.astype(F32).astype(BF16), hot_own, ((1,), (1,)))
     sel = sel_f.astype(BF16)
-    inv_two = jnp.sum(sel_f[0:2] * inv, axis=1, keepdims=True)
+    own_inv = inverse(z) * jnp.where(slot_iota < count_ref[z], 1.0, 0.0)
+    inv_two = jnp.sum(two[0:2].astype(F32) * own_inv, axis=1, keepdims=True)
     for i in range(NV):
         for p in (0, 1):
             unit_ref[:, pl.ds(FC * i + HF * p, HF)] = dot(sel, rows[i, p], ((1,), (0,)))[0:2] * inv_two
@@ -394,39 +407,38 @@
     out_ref[0:1, NV * FC : NV * FC + SLOTS] = jnp.sum(hot_own.astype(F32) * kl_col[:, :SLOTS], axis=0, keepdims=True)
     out_ref[1:2, NV * FC : NV * FC + 1] = jnp.sum(weight * kl, axis=1, keepdims=True) / TOK
 
-    mine = []
     for p in (0, 1):
         whole = collect(p, "one").astype(BF16)
-        for k, d in enumerate(PEERS_Z):
-            z_out[p, k] = dot(hot[zid(d)], whole, ((0,), (0,))).astype(BF16)
-            send("zg%d" % p, "zg%d" % p, z_out.at[p, k], z_in.at[p, k], to_z(d))
-        mine.append(dot(hot_own, whole, ((0,), (0,))))
+        spread_rows = dot(hot_t[...].reshape(NZ * SLOTS, TOK), whole, ((1,), (0,))).astype(BF16)
+        for s in range(NZ):
+            for k in range(NC):
+                at = SLOTS * s + 32 * k
+                z_out[p, NC * s + k] = spread_rows[at : at + 32]
+        for d, k in pairs:
+            to = NC * zid(d) + (c if k == 0 else other)
+            send("zg%d" % p, "zg%d" % p, z_out.at[p, to], z_in.at[p, me], to_pair(d, k))
+        z_in[p, me] = z_out[p, me]
     grads = []
     for p in (0, 1):
-        got("zg%d" % p, z_in.at[p])
-        value = mine[p]
-        for k in range(NZ - 1):
-            value = value + z_in[p, k].astype(F32)
-        grads.append(value)
-    grads = jnp.concatenate(grads, axis=1)
+        got("zg%d" % p, z_in.at[p, pl.ds(0, NP - 1)])
+        for k in range(NC):
+            value = z_in[p, k].astype(F32)
+            for s in range(1, NZ):
+                value = value + z_in[p, NC * s + k].astype(F32)
+            grads.append(value)
+    grads = jnp.concatenate([grads[0], grads[2], grads[1], grads[3]], axis=1)
     for q in range(NX * NY):
-        for cc in range(NC):
-            j = (q * NC + cc) * 2
-            tr_out[q, cc] = grads[j : j + 2]
-    for k, o in enumerate(PEERS_XY):
+        tr_out[q] = grads[2 * q : 2 * q + 2]
+    for o in PEERS_XY:
         send("tr", "tr", tr_out.at[qid(*o)], tr_in.at[q_me], to_xy(*o))
     tr_in[q_me] = tr_out[q_me]
     got("tr", tr_in.at[pl.ds(0, NX * NY - 1)])
-    send("cr", "cr", tr_in.at[:, other], tr_side, sibling)
-    got("cr", tr_side)
     both = []
     acc = jnp.zeros((2, FC), F32)
-    for q in range(NX * NY):
-        for cc in range(NC):
-            i = q * NC + cc
-            dn = jnp.where(c == cc, tr_in[q, cc], tr_side[q]) * gain(i)
-            both.append(dn)
-            acc = acc + dn * unit_ref[:, FC * i : FC * (i + 1)]
+    for i in range(NV):
+        dn = tr_in[i // 2, :, FC * (i % 2) : FC * (i % 2 + 1)] * gain(i)
+        both.append(dn)
+        acc = acc + dn * unit_ref[:, FC * i : FC * (i + 1)]
     mean = jnp.sum(acc, axis=1, keepdims=True) / (NV * FC)
     for i in range(NV):
         at = slice(FC * i, FC * (i + 1))
@@ -434,19 +446,16 @@
     for k in ("z0", "z1"):
         sent(k, zrow.at[0, pl.ds(0, NZ - 1)])
     for k in ("zt", "zs"):
-        sent(k, zt.at[pl.ds(0, NZ - 1)])
+        sent(k, zt.at[pl.ds(0, NP - 1)])
     for k in ("xt", "xs"):
         sent(k, xt.at[pl.ds(0, NX * NY - 1)])
-    for k in ("ct", "cs"):
-        sent(k, ct.at[c])
     for k in ("g", "r"):
         sent(k, rows.at[pl.ds(0, 15)])
     for k in ("cg", "cr2"):
         sent(k, rows.at[pl.ds(0, 16)])
     for k in ("zg0", "zg1"):
-        sent(k, z_out.at[0])
+        sent(k, z_out.at[0, pl.ds(0, NP - 1)])
     sent("tr", tr_out.at[pl.ds(0, NX * NY - 1)])
-    sent("cr", tr_side)
 
 
 def on_device(section_hidden, norm_gain, head, teacher_logits, exit_layer, row_count, row_index):
@@ -465,13 +474,13 @@
             pltpu.VMEM((NV, FC, TOK), BF16),
             pltpu.VMEM((NV, 2, TOK, HF), BF16),
             pltpu.VMEM((2, NZ, SLOTS, HF), BF16),
-            pltpu.VMEM((NZ, 4, TOK), F32),
-            pltpu.VMEM((NZ, 4, TOK), F32),
+            pltpu.VMEM((NP, 4, TOK), F32),
+            pltpu.VMEM((NP, 4, TOK), F32),
             pltpu.VMEM((NX * NY, 4, TOK), F32),
             pltpu.VMEM((NX * NY, 4, TOK), F32),
-            pltpu.VMEM((NC, 4, TOK), F32),
-            pltpu.VMEM((NC, 4, TOK), F32),
             pltpu.VMEM((NZ, TOK, SLOTS), BF16),
+            pltpu.VMEM((TOK, NZ * SLOTS), BF16),
+            pltpu.VMEM((NZ, SLOTS, TOK), BF16),
             pltpu.VMEM((16, 2, TOK, HF), BF16),
             pltpu.VMEM((16, 2, TOK, HF), BF16),
             pltpu.VMEM((16, 2, TOK, HF), F32),
@@ -479,11 +488,10 @@
             pltpu.VMEM((2, 5, 2, HT, HF), BF16),
             pltpu.VMEM((2, 5, 3, TOK, HF), BF16),
             pltpu.VMEM((2, 5, 3, TOK, HF), BF16),
-            pltpu.VMEM((2, NZ - 1, SLOTS, HF), BF16),
-            pltpu.VMEM((2, NZ - 1, SLOTS, HF), BF16),
-            pltpu.VMEM((16, 2, 2, FC), F32),
-            pltpu.VMEM((16, 2, 2, FC), F32),
-            pltpu.VMEM((16, 2, FC), F32),
+            pltpu.VMEM((2, NP, 32, HF), BF16),
+            pltpu.VMEM((2, NP, 32, HF), BF16),
+            pltpu.VMEM((NX * NY, 2, NC * FC), F32),
+            pltpu.VMEM((NX * NY, 2, NC * FC), F32),
             pltpu.VMEM((2, NV * FC), F32),
             pltpu.VMEM((TOK, 256), F32),
             pltpu.SemaphoreType.DMA((6,)),

time: 81.6 us -> 77.1 us (0.945)
  Pallas kernels: 79.2 us -> 74.7 us
    pallas_call x1, Pallas kernels: 79.2 us -> 74.7 us  [on_device(): pl.pallas_call(kernel, out_shape=pltpu.VMEM((2, NV * FC + 128), F32), in_...]
where the time goes in v3:
time: 77.1 us; the launch traced here: 77 us
  Pallas kernels  74.7 us (97%)
  local copies, waits for them, and re-layouts  1.66 us (2%)
    pallas_call x1, Pallas kernels, on_device(): pl.pallas_call(kernel, out_shape=pltpu.VMEM((2, NV * FC + 128), F32), in_...  74.7 us

profile of v3, /device:TPU:1, one launch (start us, length us, event | category | flops | bytes accessed | tf_op | source)
XLA Modules:
  0.0 77.0 jit_solution(13027530990987887276)
XLA Ops:
  0.6 74.7 %exit_loss.1 = f32[2,8320]{1,0:T(2,128)S(1)} custom-call(bf16[1,256,256]{2,1,0:T(8,128)(2,1)} %hidden_hbm.1, f32[64,128]{1,0:T(8,128)} %bitcast.7, bf16[32,256,256]{2,1,0:T(8,128)(2,1)} %bitcast.6, bf16[256,256]{1,0:T(8,128)(2,1)} %teacher_hbm.1, s32[1,256]{1,0:T(1,128)} %bitcast.8, s32[8]{0:T(128)} %count_hbm.1, s32[8,64]{1,0:T(8,128)} %index_hbm.1), custom_call_target="tpu_custom_call" | custom-call | tf_op jit(solution)/shard_map/exit_loss/pallas_call | solution.py:462
  75.3 0.5 slice.11
  75.8 0.5 slice.10
  76.3 0.6 fusion

commit v4 on v3

--- a/solution.py
+++ b/solution.py
@@ -26,19 +26,18 @@
 FAR = [(2, 2), (2, 1), (1, 2), (2, -1), (-1, 2), (2, 0), (0, 2), (1, 1), (-1, 1), (1, -1), (-1, -1), (0, 1), (1, 0), (0, -1), (-1, 0), (0, 0)]
 
 
-RING_G = (0, 1, -1)
-RING_R = (0,)
+RING_G = ((0,), (0,))
+RING_R = ((0,), (0,))
 
 
 def all_names():
-    names = ["z0", "z1", "zt", "xt", "zs", "xs", "zg0", "zg1", "tr"]
+    names = ["z0", "z1", "zt", "xt", "zs", "xs", "zg0", "zg1", "tr", "hd", "st", "tc", "un"]
     names += [("ring", p, d, k) for p in (0, 1) for d in OFFS + ("one",) for k in range(3)]
-    names += [("core", o) for o in PLANE]
     return {k: i for i, k in enumerate(names)}
 
 
 NAMES = all_names()
-GROUPS = {k: i for i, k in enumerate(["z0", "z1", "zt", "xt", "zs", "xs", "zg0", "zg1", "tr", "g", "r", "cg", "cr2"])}
+GROUPS = {k: i for i, k in enumerate(["z0", "z1", "zt", "xt", "zs", "xs", "zg0", "zg1", "tr", "g", "r", "hd", "st", "tc", "un"])}
 
 
 def dot(a, b, dims):
@@ -50,9 +49,9 @@
     out_ref,
     hidden_ref, gain_ref, teacher_ref, layer_ref, count_ref, index_ref, head,
     rows, zrow, zt, zs, xt, xs,
-    hot, hot_all, hot_t, cross_out, cross_in, part_sum, half_out, half_in, full_out, full_in,
-    z_out, z_in, tr_out, tr_in, unit_ref,
-    stu, load_sem, head_sem, send_sem, recv_sem,
+    hot, hot_all, hot_t, teacher_sib, part_sum, half_out, half_in, full_out, full_in,
+    z_out, z_in, tr_out, tr_in, unit_own, unit_out, unit_sib,
+    stu, stu_in, load_sem, head_sem, send_sem, recv_sem,
 ):
     z = lax.axis_index("section")
     v = lax.axis_index("vocab")
@@ -104,7 +103,7 @@
         pl.semaphore_signal(barrier, inc=1, device_id=t, device_id_type=MESH)
     small = [(index_hbm, index_ref), (hidden_hbm, hidden_ref), (teacher_hbm, teacher_ref), (count_hbm, count_ref), (gain_hbm, gain_ref), (layer_hbm, layer_ref)]
     small = [pltpu.make_async_copy(a, b, load_sem.at[i]) for i, (a, b) in enumerate(small)]
-    loads = [pltpu.make_async_copy(head_hbm.at[pl.ds(8 * i, 8)], head.at[pl.ds(8 * i, 8)], head_sem.at[i]) for i in range(4)]
+    loads = [pltpu.make_async_copy(head_hbm.at[pl.ds(4 * i, 4), c], head.at[pl.ds(4 * i, 4), :, pl.ds(0, FC)], head_sem.at[i]) for i in range(4)]
     for cp in small + loads:
         cp.start()
     for cp in small:
@@ -123,9 +122,8 @@
     q_me = qid(0, 0)
     tea = teacher_ref[...].astype(F32).T
     top = jnp.max(tea, axis=0, keepdims=True)
-    xt[q_me, 0:1] = top
-    xt[q_me, 1:2] = jnp.sum(jnp.exp(tea - top), axis=0, keepdims=True)
-    xt[q_me, 2:3, 0:SLOTS] = jnp.sum(squares, axis=0, keepdims=True)
+    xt[q_me, 0:1] = top + jnp.log(jnp.sum(jnp.exp(tea - top), axis=0, keepdims=True))
+    xt[q_me, 1:2, 0:SLOTS] = jnp.sum(squares, axis=0, keepdims=True)
     for s in range(NZ):
         live_row = jnp.where(slot_iota < count_ref[s], index_ref[s : s + 1, :], -1)
         hot[s] = (tok_iota == live_row).astype(F32).astype(BF16)
@@ -138,6 +136,10 @@
     for d in PEERS_Z:
         send("z1", "z1", zrow.at[1, z], zrow.at[1, z], to_z(d))
 
+    head_side = head.at[:, :, pl.ds(FC, FC)]
+    send("tc", "tc", teacher_ref, teacher_sib, sibling)
+    send("hd", "hd", head_hbm.at[:, other], head_side, sibling)
+
     row = lax.broadcasted_iota(jnp.int32, (SLOTS, SLOTS), 0)
     col = lax.broadcasted_iota(jnp.int32, (SLOTS, SLOTS), 1)
     perm = (row == 4 * ((col % 32) // 2) + 2 * (col // 32) + col % 2).astype(F32).astype(BF16)
@@ -153,58 +155,51 @@
     def axis2(p, d):
         return to_xy(0, d) if p == 0 else to_xy(d, 0)
 
-    def block(p, o, h=None, core=None):
-        at = vid(*o, c if core is None else core)
+    def block(p, o, h=None):
+        at = qid(*o)
         if h is None:
             return rows.at[at, p]
         return rows.at[at, p, pl.ds(HT * h, HT)]
 
-    def relay(p, o):
-        send("cg", ("core", o), block(p, o), block(p, o), sibling)
-
     sides = ((0, -1, 1), (1, 1, -1))
 
     def spread(p, d, o, axis):
         send("g", ("ring", p, d, 0), block(p, o), block(p, o), axis(p, 1))
         send("g", ("ring", p, d, 1), block(p, o), block(p, o), axis(p, -1))
-        if d not in RING_G:
+        if d not in RING_G[p]:
             send("g", ("ring", p, d, 2), block(p, o), block(p, o), axis(p, 2))
 
     def forward(p, d, o, s, axis):
-        if d in RING_G:
+        if d in RING_G[p]:
             send("g", ("ring", p, d, 2), block(p, o, s), block(p, o, s), axis(p, sides[s][2]))
 
-    def merge(buf, n, at):
-        m = buf[0, at : at + 1]
-        for i in range(1, n):
-            m = jnp.maximum(m, buf[i, at : at + 1])
-        t = jnp.zeros_like(m)
-        for i in range(n):
-            t = t + buf[i, at + 1 : at + 2] * jnp.exp(buf[i, at : at + 1] - m)
-        return m, t
-
-    def total(buf, n, at):
-        t = buf[0, at : at + 1]
-        for i in range(1, n):
-            t = t + buf[i, at : at + 1]
-        return t
-
-    have = {(0, 0): 2}
-    ready = []
+    def tree(op, values):
+        while len(values) > 1:
+            values = [op(*values[i : i + 2]) if i + 1 < len(values) else values[i] for i in range(0, len(values), 2)]
+        return values[0]
+
+    def merge(buf, n):
+        each = [buf[i, 0:1] for i in range(n)]
+        m = tree(jnp.maximum, each)
+        return m + jnp.log(tree(jnp.add, [jnp.exp(e - m) for e in each]))
+
+    def total(buf, n):
+        return tree(jnp.add, [buf[i, 1:2] for i in range(n)])
+
+    have = {}
+    ready = [(0, 0)]
 
     def arrived(p, o):
-        relay(p, o)
         have[o] = have.get(o, 0) + 1
         if have[o] == 2:
-            ready.append((o, c))
+            ready.append(o)
 
     def start(p):
         got("z%d" % p, zrow.at[p, pl.ds(0, NZ - 1)])
         mine = dot(hot_all[...], zrow[p].reshape(NZ * SLOTS, HF), ((1,), (0,)))
-        rows[v, p] = mine.astype(BF16)
+        rows[q_me, p] = mine.astype(BF16)
         spread(p, "one", (0, 0), axis1)
         spread(p, 0, (0, 0), axis2)
-        relay(p, (0, 0))
 
     def first(p):
         for s, frm, to in sides:
@@ -225,10 +220,8 @@
 
     start(0)
     got("xt", xt.at[pl.ds(0, NX * NY - 1)])
-    m, t = merge(xt, NX * NY, 0)
-    zt[me, 0:1] = m
-    zt[me, 1:2] = t
-    zt[me, 2:3] = total(xt, NX * NY, 2)
+    zt[me, 0:1] = merge(xt, NX * NY)
+    zt[me, 1:2] = total(xt, NX * NY)
     for o in pairs:
         send("zt", "zt", zt.at[me], zt.at[me], to_pair(*o))
     start(1)
@@ -238,38 +231,25 @@
     for cp in loads:
         cp.wait()
     got("zt", zt.at[pl.ds(0, NP - 1)])
-    m, t = merge(zt, NP, 0)
-    lse_t = m + jnp.log(t)
+    lse_t = merge(zt, NP)
     spots = jnp.zeros((TOK, SLOTS), F32)
 
     def inverse(s):
-        return lax.rsqrt((zt[NC * s, 2:3, 0:SLOTS] + zt[NC * s + 1, 2:3, 0:SLOTS]) / (NV * FC) + EPS)
+        return lax.rsqrt((zt[NC * s, 1:2, 0:SLOTS] + zt[NC * s + 1, 1:2, 0:SLOTS]) / (NV * FC) + EPS)
 
     for s in range(NZ):
         spots = spots + hot[s].astype(F32) * inverse(s)
     inv_wide = jnp.broadcast_to(jnp.sum(spots, axis=1, keepdims=True), (TOK, FC))
 
-    def score(chunk):
-        raw = jnp.concatenate([rows[chunk, 0], rows[chunk, 1]], axis=1)
-        normed = (raw.astype(F32) * inv_wide * gain(chunk)).astype(BF16)
-        stu[...] += dot(normed, head[chunk], ((1,), (0,)))
-
-    def score_sibling(o):
-        got(("core", o), rows.at[vid(*o, other)])
-        score(vid(*o, other))
-
-    scored = []
-
-    def drain(lag):
+    def drain():
         while ready:
-            o, _ = ready.pop(0)
-            score(vid(*o, c))
-            scored.append(o)
-        while len(scored) > lag:
-            score_sibling(scored.pop(0))
-
-    ready.insert(0, ((0, 0), c))
-    drain(4)
+            q = qid(*ready.pop(0))
+            raw = jnp.concatenate([rows[q, 0], rows[q, 1]], axis=1)
+            normed = (raw.astype(F32) * inv_wide * gain(NC * q + c)).astype(BF16)
+            stu[...] += dot(normed, head[q], ((1,), (0,)))
+
+    got("hd", head_side)
+    drain()
     for d in (1, -1):
         for p in (0, 1):
             for s, frm, to in sides:
@@ -277,7 +257,9 @@
                 got(("ring", p, d, s), block(p, o))
                 forward(p, d, o, s, axis2)
                 arrived(p, o)
-        drain(4)
+        drain()
+    got("tc", teacher_sib)
+    tea = jnp.concatenate([tea, teacher_sib[...].astype(F32).T], axis=0)
     prob = jnp.exp(tea - lse_t)
     weight = (layer_ref[...].astype(F32) + 1.0) / LAYERS
     for d in (0, 2, 1, -1):
@@ -291,30 +273,24 @@
             o = off(p, d, 2)
             got(("ring", p, d, 2), block(p, o))
             arrived(p, o)
-        drain(3)
-    drain(0)
-    student = stu[...].T
+        drain()
+    send("st", "st", stu, stu_in, sibling)
+    got("st", stu_in)
+    student = jnp.concatenate([(stu[:, :FC] + stu_in[:, FC:]).T, (stu[:, FC:] + stu_in[:, :FC]).T], axis=0)
     m = jnp.max(student, axis=0, keepdims=True)
-    zs[me, 0:1] = m
-    zs[me, 1:2] = jnp.sum(jnp.exp(student - m), axis=0, keepdims=True)
-    zs[me, 2:3] = jnp.sum(prob * (tea - student), axis=0, keepdims=True)
-    for o in pairs:
-        send("zs", "zs", zs.at[me], zs.at[me], to_pair(*o))
-    got("zs", zs.at[pl.ds(0, NP - 1)])
-    m, t = merge(zs, NP, 0)
-    xs[q_me, 0:1] = m
-    xs[q_me, 1:2] = t
-    xs[q_me, 2:3] = total(zs, NP, 2)
+    zs[z, 0:1] = m + jnp.log(jnp.sum(jnp.exp(student - m), axis=0, keepdims=True))
+    zs[z, 1:2] = jnp.sum(prob * (tea - student), axis=0, keepdims=True)
+    for d in PEERS_Z:
+        send("zs", "zs", zs.at[z], zs.at[z], to_z(d))
+    got("zs", zs.at[pl.ds(0, NZ - 1)])
+    xs[q_me, 0:1] = merge(zs, NZ)
+    xs[q_me, 1:2] = total(zs, NZ)
     for o in PEERS_XY:
         send("xs", "xs", xs.at[q_me], xs.at[q_me], to_xy(*o))
     got("xs", xs.at[pl.ds(0, NX * NY - 1)])
-    m, t = merge(xs, NX * NY, 0)
-    lse_s = m + jnp.log(t)
-    kl = total(xs, NX * NY, 2) - lse_t + lse_s
+    lse_s = merge(xs, NX * NY)
+    kl = total(xs, NX * NY) - lse_t + lse_s
     dlogit = (weight * (jnp.exp(student - lse_s) - prob)).T.astype(BF16)
-    def part(chunk):
-        return dot(dlogit, head[chunk], ((1,), (1,)))
-
     def own(o):
         return PLANE.index(o)
 
@@ -326,7 +302,7 @@
 
     def give(p, d, d1, axis, value):
         i, k = chunk_at(p, d, d1), slot(d)
-        if d1 != 0 and d not in RING_R:
+        if d1 != 0 and d not in RING_R[p]:
             j = (1, -1, 2).index(d1)
             full_out[p, k, j] = value.astype(BF16)
             send("r", ("ring", p, d, 2), full_out.at[p, k, j], full_in.at[p, k, j], axis(p, d1))
@@ -338,7 +314,7 @@
             part_sum[i, p] = value
 
     def pass_on(p, d, axis):
-        if d not in RING_R:
+        if d not in RING_R[p]:
             return
         k = slot(d)
         for s in (0, 1):
@@ -352,31 +328,18 @@
 
     def collect(p, d):
         i, k = chunk_at(p, d, 0), slot(d)
-        n = 2 if d in RING_R else 3
+        n = 2 if d in RING_R[p] else 3
         got(("ring", p, d, 2), full_in.at[p, k, pl.ds(0, n)])
         value = part_sum[i, p]
         for j in range(n):
             value = value + full_in[p, k, j].astype(F32)
         return value
 
-    def settle(o):
-        i = own(o)
-        value = part(vid(*o, c))
-        got(("core", o), cross_in.at[i])
+    for o in FAR:
+        value = dot(dlogit, head[qid(*o)], ((1,), (1,)))
         for p in (0, 1):
             d1, d2 = o[::-1] if p == 0 else o
-            give(p, d2, d1, axis2, value[:, HF * p : HF * (p + 1)] + cross_in[i, p].astype(F32))
-
-    lag = 3
-    for k, o in enumerate(FAR):
-        value = part(vid(*o, other)).astype(BF16)
-        for p in (0, 1):
-            cross_out[own(o), p] = value[:, HF * p : HF * (p + 1)]
-        send("cr2", ("core", o), cross_out.at[own(o)], cross_in.at[own(o)], sibling)
-        if k >= lag:
-            settle(FAR[k - lag])
-    for o in FAR[-lag:]:
-        settle(o)
+            give(p, d2, d1, axis2, value[:, HF * p : HF * (p + 1)])
 
     for d in (2, 1, -1):
         for p in (0, 1):
@@ -395,14 +358,20 @@
         part_sum[own((0, 0)), p] = collect(p, 0)
 
     hot_own = hot[z]
-    two = lax.broadcasted_iota(jnp.int32, (16, SLOTS), 0) + 2 * v == lax.broadcasted_iota(jnp.int32, (16, SLOTS), 1)
-    sel_f = dot(two.astype(F32).astype(BF16), hot_own, ((1,), (1,)))
-    sel = sel_f.astype(BF16)
+    pick4 = lax.broadcasted_iota(jnp.int32, (16, SLOTS), 0)
+    pick4 = jnp.where(pick4 < 2, 2 * v + pick4, 2 * vid(0, 0, other) + pick4 - 2)
+    pick4 = (pick4 == lax.broadcasted_iota(jnp.int32, (16, SLOTS), 1)).astype(F32)
+    sel = dot(pick4.astype(BF16), hot_own, ((1,), (1,))).astype(BF16)
     own_inv = inverse(z) * jnp.where(slot_iota < count_ref[z], 1.0, 0.0)
-    inv_two = jnp.sum(two[0:2].astype(F32) * own_inv, axis=1, keepdims=True)
-    for i in range(NV):
-        for p in (0, 1):
-            unit_ref[:, pl.ds(FC * i + HF * p, HF)] = dot(sel, rows[i, p], ((1,), (0,)))[0:2] * inv_two
+    inv_four = jnp.sum(pick4[0:4] * own_inv, axis=1, keepdims=True)
+    inv_two = inv_four[0:2]
+    for q in range(NX * NY):
+        for p in (0, 1):
+            four = dot(sel, rows[q, p], ((1,), (0,)))[0:4] * inv_four
+            at = slice(FC * q + HF * p, FC * q + HF * (p + 1))
+            unit_own[:, at] = four[0:2]
+            unit_out[:, at] = four[2:4]
+    send("un", "un", unit_out, unit_sib, sibling)
     kl_col = jnp.broadcast_to(kl, (HF, TOK)).T
     out_ref[0:1, NV * FC : NV * FC + SLOTS] = jnp.sum(hot_own.astype(F32) * kl_col[:, :SLOTS], axis=0, keepdims=True)
     out_ref[1:2, NV * FC : NV * FC + 1] = jnp.sum(weight * kl, axis=1, keepdims=True) / TOK
@@ -433,26 +402,30 @@
         send("tr", "tr", tr_out.at[qid(*o)], tr_in.at[q_me], to_xy(*o))
     tr_in[q_me] = tr_out[q_me]
     got("tr", tr_in.at[pl.ds(0, NX * NY - 1)])
+    got("un", unit_sib)
     both = []
+    units = []
     acc = jnp.zeros((2, FC), F32)
     for i in range(NV):
-        dn = tr_in[i // 2, :, FC * (i % 2) : FC * (i % 2 + 1)] * gain(i)
-        both.append(dn)
-        acc = acc + dn * unit_ref[:, FC * i : FC * (i + 1)]
+        at = slice(FC * (i // 2), FC * (i // 2 + 1))
+        units.append(jnp.where(c == i % 2, unit_own[:, at], unit_sib[:, at]))
+        both.append(tr_in[i // 2, :, FC * (i % 2) : FC * (i % 2 + 1)] * gain(i))
+        acc = acc + both[i] * units[i]
     mean = jnp.sum(acc, axis=1, keepdims=True) / (NV * FC)
     for i in range(NV):
-        at = slice(FC * i, FC * (i + 1))
-        out_ref[:, at] = inv_two * (both[i] - unit_ref[:, at] * mean)
+        out_ref[:, FC * i : FC * (i + 1)] = inv_two * (both[i] - units[i] * mean)
     for k in ("z0", "z1"):
         sent(k, zrow.at[0, pl.ds(0, NZ - 1)])
-    for k in ("zt", "zs"):
-        sent(k, zt.at[pl.ds(0, NP - 1)])
+    sent("zt", zt.at[pl.ds(0, NP - 1)])
+    sent("zs", zt.at[pl.ds(0, NZ - 1)])
     for k in ("xt", "xs"):
         sent(k, xt.at[pl.ds(0, NX * NY - 1)])
     for k in ("g", "r"):
         sent(k, rows.at[pl.ds(0, 15)])
-    for k in ("cg", "cr2"):
-        sent(k, rows.at[pl.ds(0, 16)])
+    sent("hd", head_side)
+    sent("st", stu_in)
+    sent("tc", teacher_sib)
+    sent("un", unit_out)
     for k in ("zg0", "zg1"):
         sent(k, z_out.at[0, pl.ds(0, NP - 1)])
     sent("tr", tr_out.at[pl.ds(0, NX * NY - 1)])
@@ -471,19 +444,18 @@
             pltpu.VMEM((1, TOK), jnp.int32),
             pltpu.SMEM((NZ,), jnp.int32),
             pltpu.VMEM((NZ, SLOTS), jnp.int32),
-            pltpu.VMEM((NV, FC, TOK), BF16),
-            pltpu.VMEM((NV, 2, TOK, HF), BF16),
+            pltpu.VMEM((NX * NY, FC, NC * FC), BF16),
+            pltpu.VMEM((NX * NY, 2, TOK, HF), BF16),
             pltpu.VMEM((2, NZ, SLOTS, HF), BF16),
-            pltpu.VMEM((NP, 4, TOK), F32),
-            pltpu.VMEM((NP, 4, TOK), F32),
-            pltpu.VMEM((NX * NY, 4, TOK), F32),
-            pltpu.VMEM((NX * NY, 4, TOK), F32),
+            pltpu.VMEM((NP, 2, TOK), F32),
+            pltpu.VMEM((NZ, 2, TOK), F32),
+            pltpu.VMEM((NX * NY, 2, TOK), F32),
+            pltpu.VMEM((NX * NY, 2, TOK), F32),
             pltpu.VMEM((NZ, TOK, SLOTS), BF16),
             pltpu.VMEM((TOK, NZ * SLOTS), BF16),
             pltpu.VMEM((NZ, SLOTS, TOK), BF16),
-            pltpu.VMEM((16, 2, TOK, HF), BF16),
-            pltpu.VMEM((16, 2, TOK, HF), BF16),
-            pltpu.VMEM((16, 2, TOK, HF), F32),
+            pltpu.VMEM((TOK, FC), BF16),
+            pltpu.VMEM((NX * NY, 2, TOK, HF), F32),
             pltpu.VMEM((2, 5, 2, HT, HF), BF16),
             pltpu.VMEM((2, 5, 2, HT, HF), BF16),
             pltpu.VMEM((2, 5, 3, TOK, HF), BF16),
@@ -492,8 +464,11 @@
             pltpu.VMEM((2, NP, 32, HF), BF16),
             pltpu.VMEM((NX * NY, 2, NC * FC), F32),
             pltpu.VMEM((NX * NY, 2, NC * FC), F32),
-            pltpu.VMEM((2, NV * FC), F32),
-            pltpu.VMEM((TOK, 256), F32),
+            pltpu.VMEM((2, NX * NY * FC), F32),
+            pltpu.VMEM((2, NX * NY * FC), F32),
+            pltpu.VMEM((2, NX * NY * FC), F32),
+            pltpu.VMEM((TOK, NC * FC), F32),
+            pltpu.VMEM((TOK, NC * FC), F32),
             pltpu.SemaphoreType.DMA((6,)),
             pltpu.SemaphoreType.DMA((4,)),
             pltpu.SemaphoreType.DMA((len(GROUPS),)),
@@ -504,7 +479,7 @@
     )(
         section_hidden,
         norm_gain.reshape(2 * NV, 128),
-        head.reshape(NV, FC, head.shape[1]),
+        head.reshape(NX * NY, NC, FC, head.shape[1]),
         teacher_logits,
         exit_layer.reshape(1, TOK),
         row_count,

time: 77.1 us -> 75.4 us (0.978)
  Pallas kernels: 74.7 us -> 73 us
    pallas_call x1, Pallas kernels: 74.7 us -> 73 us  [on_device(): pl.pallas_call(kernel, out_shape=pltpu.VMEM((2, NV * FC + 128), F32), in_...]
where the time goes in v4:
time: 75.4 us; the launch traced here: 75.3 us
  Pallas kernels  73 us (97%)
  local copies, waits for them, and re-layouts  1.66 us (2%)
    pallas_call x1, Pallas kernels, on_device(): pl.pallas_call(kernel, out_shape=pltpu.VMEM((2, NV * FC + 128), F32), in_...  73 us

profile of v4, /device:TPU:1, one launch (start us, length us, event | category | flops | bytes accessed | tf_op | source)
XLA Modules:
  0.0 75.3 jit_solution(2807314082878887949)
XLA Ops:
  0.6 73.0 %exit_loss.1 = f32[2,8320]{1,0:T(2,128)S(1)} custom-call(bf16[1,256,256]{2,1,0:T(8,128)(2,1)} %hidden_hbm.1, f32[64,128]{1,0:T(8,128)} %bitcast.7, bf16[16,2,256,256]{3,2,1,0:T(8,128)(2,1)} %bitcast.6, bf16[256,256]{1,0:T(8,128)(2,1)} %teacher_hbm.1, s32[1,256]{1,0:T(1,128)} %bitcast.8, s32[8]{0:T(128)} %count_hbm.1, s32[8,64]{1,0:T(8,128)} %index_hbm.1), custom_call_target="tpu_custom_call" | custom-call | tf_op jit(solution)/shard_map/exit_loss/pallas_call | solution.py:435
  73.6 0.5 slice.11
  74.1 0.5 slice.10
  74.6 0.6 fusion

commit v5 on v4

--- a/solution.py
+++ b/solution.py
@@ -138,7 +138,6 @@
 
     head_side = head.at[:, :, pl.ds(FC, FC)]
     send("tc", "tc", teacher_ref, teacher_sib, sibling)
-    send("hd", "hd", head_hbm.at[:, other], head_side, sibling)
 
     row = lax.broadcasted_iota(jnp.int32, (SLOTS, SLOTS), 0)
     col = lax.broadcasted_iota(jnp.int32, (SLOTS, SLOTS), 1)
@@ -225,6 +224,7 @@
     for o in pairs:
         send("zt", "zt", zt.at[me], zt.at[me], to_pair(*o))
     start(1)
+    send("hd", "hd", head_hbm.at[:, other], head_side, sibling)
     first(0)
     first(1)
     stu[...] = jnp.zeros_like(stu)

time: 75.4 us -> 75.4 us (level)
  no operation moved by 1% of the time
where the time goes in v5:
time: 75.4 us; the launch traced here: 75.3 us
  Pallas kernels  73 us (97%)
  local copies, waits for them, and re-layouts  1.66 us (2%)
    pallas_call x1, Pallas kernels, on_device(): pl.pallas_call(kernel, out_shape=pltpu.VMEM((2, NV * FC + 128), F32), in_...  73 us

profile of v5, /device:TPU:1, one launch (start us, length us, event | category | flops | bytes accessed | tf_op | source)
XLA Modules:
  0.0 75.3 jit_solution(1357754601513730262)
XLA Ops:
  0.6 73.0 %exit_loss.1 = f32[2,8320]{1,0:T(2,128)S(1)} custom-call(bf16[1,256,256]{2,1,0:T(8,128)(2,1)} %hidden_hbm.1, f32[64,128]{1,0:T(8,128)} %bitcast.7, bf16[16,2,256,256]{3,2,1,0:T(8,128)(2,1)} %bitcast.6, bf16[256,256]{1,0:T(8,128)(2,1)} %teacher_hbm.1, s32[1,256]{1,0:T(1,128)} %bitcast.8, s32[8]{0:T(128)} %count_hbm.1, s32[8,64]{1,0:T(8,128)} %index_hbm.1), custom_call_target="tpu_custom_call" | custom-call | tf_op jit(solution)/shard_map/exit_loss/pallas_call | solution.py:435
  73.6 0.5 slice.11
  74.1 0.5 slice.10
  74.6 0.6 fusion

commit v6 on v5

--- a/solution.py
+++ b/solution.py
@@ -207,15 +207,19 @@
             forward(p, "one", o, s, axis1)
             spread(p, frm, o, axis2)
             arrived(p, o)
+
+    def second(p):
+        o = off(p, 2, 0)
+        got(("ring", p, "one", 2), block(p, o))
+        spread(p, 2, o, axis2)
+        arrived(p, o)
+
+    def third(p):
         for s, frm, to in sides:
             o = off(p, 0, frm)
             got(("ring", p, 0, s), block(p, o))
             forward(p, 0, o, s, axis2)
             arrived(p, o)
-        o = off(p, 2, 0)
-        got(("ring", p, "one", 2), block(p, o))
-        spread(p, 2, o, axis2)
-        arrived(p, o)
 
     start(0)
     got("xt", xt.at[pl.ds(0, NX * NY - 1)])
@@ -226,7 +230,11 @@
     start(1)
     send("hd", "hd", head_hbm.at[:, other], head_side, sibling)
     first(0)
+    second(0)
+    third(0)
     first(1)
+    second(1)
+    third(1)
     stu[...] = jnp.zeros_like(stu)
     for cp in loads:
         cp.wait()

time: 75.4 us -> 75.2 us (level)
  no operation moved by 1% of the time
where the time goes in v6:
time: 75.2 us; the launch traced here: 75.1 us
  Pallas kernels  72.8 us (97%)
  local copies, waits for them, and re-layouts  1.66 us (2%)
    pallas_call x1, Pallas kernels, on_device(): pl.pallas_call(kernel, out_shape=pltpu.VMEM((2, NV * FC + 128), F32), in_...  72.8 us

profile of v6, /device:TPU:1, one launch (start us, length us, event | category | flops | bytes accessed | tf_op | source)
XLA Modules:
  0.0 75.1 jit_solution(6227881247173128355)
XLA Ops:
  0.6 72.8 %exit_loss.1 = f32[2,8320]{1,0:T(2,128)S(1)} custom-call(bf16[1,256,256]{2,1,0:T(8,128)(2,1)} %hidden_hbm.1, f32[64,128]{1,0:T(8,128)} %bitcast.7, bf16[16,2,256,256]{3,2,1,0:T(8,128)(2,1)} %bitcast.6, bf16[256,256]{1,0:T(8,128)(2,1)} %teacher_hbm.1, s32[1,256]{1,0:T(1,128)} %bitcast.8, s32[8]{0:T(128)} %count_hbm.1, s32[8,64]{1,0:T(8,128)} %index_hbm.1), custom_call_target="tpu_custom_call" | custom-call | tf_op jit(solution)/shard_map/exit_loss/pallas_call | solution.py:443
  73.5 0.5 slice.11
  74.0 0.5 slice.10
  74.5 0.6 fusion
